TPU v7x, 256 devices: a whole 4x4x8 slice. The times are simulated.
256 devices in a mesh: row: 16 (over y, x_hi, core), col: 16 (over z, x_lo).
Axes of the slice: x: 4 (x_hi: 2, x_lo: 2; x = x_hi * 2 + x_lo), y: 4, z: 8, core: 2. Of those that a mesh axis runs over, the one named last changes fastest.
Arguments:
- pair: bfloat16 [512, 512, 128], P('row', 'col'), may hold values from -1.5 to 1.5
- norm_gain: float32 [3, 128], replicated, may hold values from 0.1 to 1.9
- norm_bias: float32 [3, 128], replicated, may hold values from -3 to 3
- proj_weight: bfloat16 [2, 128, 640], replicated, may hold values from -0.5 to 0.5
- out_gain: float32 [2, 128], replicated, may hold values from 0.1 to 1.9
- out_bias: float32 [2, 128], replicated, may hold values from -3 to 3
- out_weight: bfloat16 [2, 128, 128], replicated, may hold values from -1 to 1
- up_weight: bfloat16 [128, 1024], replicated, may hold values from -0.5 to 0.5
- down_weight: bfloat16 [512, 128], replicated, may hold values from -0.25 to 0.25
Outputs:
- updated: bfloat16 [512, 512, 128], P('row', 'col')
All inputs are finite; a program needn't handle non-finite values.
Results may differ from a plain program's by a relative error of at most 0.029.
Values may be sent and summed in bfloat16 or wider, within the bound.
No kernel may reach another device: no remote copies, remote signals or barrier semaphores. Data moves between devices by JAX's collectives and lax.ppermute only.
A program may use at most 128 MiB of HBM per device.

v0:
```python
import jax
import jax.numpy as jnp
from jax import lax
from jax.sharding import PartitionSpec as P


def spread(value, axis, source):
    kept = jnp.where(lax.axis_index(axis) == source, value, 0).astype(value.dtype)
    return lax.psum(kept, axis)


def layer_norm(values, gain, bias):
    mean = jnp.mean(values, axis=-1, keepdims=True)
    centred = values - mean
    var = jnp.mean(centred * centred, axis=-1, keepdims=True)
    return centred * lax.rsqrt(var + 1e-05) * gain + bias


def prepare(field, gain, bias, weight, hidden):
    rows, cols, width = field.shape
    normed = layer_norm(field, gain, bias).astype(jnp.bfloat16).reshape(rows * cols, width)
    proj = jnp.dot(normed, weight, preferred_element_type=jnp.float32).reshape(rows, cols, -1)
    left = (jax.nn.sigmoid(proj[..., :hidden]) * proj[..., hidden : 2 * hidden]).astype(
        jnp.bfloat16
    )
    right = (
        jax.nn.sigmoid(proj[..., 2 * hidden : 3 * hidden]) * proj[..., 3 * hidden : 4 * hidden]
    ).astype(jnp.bfloat16)
    gate = jax.nn.sigmoid(proj[..., 4 * hidden :])
    return (left, right, gate)


def finish(field, mixed, gain, bias, weight, gate):
    mixnorm = layer_norm(mixed, gain, bias).astype(jnp.bfloat16)
    branch = jnp.einsum("ijh,hc->ijc", mixnorm, weight, preferred_element_type=jnp.float32)
    return field + gate * branch


def body(
    pair, norm_gain, norm_bias, proj_weight, out_gain, out_bias, out_weight, up_weight, down_weight
):
    hidden = out_weight.shape[1]
    ratio = lax.axis_size("row") // lax.axis_size("col")
    field = pair.astype(jnp.float32)
    left, right, gate = prepare(field, norm_gain[0], norm_bias[0], proj_weight[0], hidden)
    left_rows, right_rows = (
        lax.all_gather(left, "col", axis=1, tiled=True),
        lax.all_gather(right, "col", axis=1, tiled=True),
    )
    owner = lax.axis_index("col") * ratio
    pieces = spread(right_rows, "row", owner + 0)
    mixed = jnp.einsum("ikc,jkc->ijc", left_rows, pieces, preferred_element_type=jnp.float32)
    field = finish(field, mixed, out_gain[0], out_bias[0], out_weight[0], gate)
    left, right, gate = prepare(field, norm_gain[1], norm_bias[1], proj_weight[1], hidden)
    left_cols, right_cols = (
        lax.all_gather(left, "row", axis=0, tiled=True),
        lax.all_gather(right, "row", axis=0, tiled=True),
    )
    row_index = lax.axis_index("row")
    held = spread(left_cols, "col", row_index // ratio)
    mixed = jnp.einsum("kic,kjc->ijc", held, right_cols, preferred_element_type=jnp.float32)
    field = finish(field, mixed, out_gain[1], out_bias[1], out_weight[1], gate)
    rows, cols, width = field.shape
    inner = down_weight.shape[0]
    tnorm = (
        layer_norm(field, norm_gain[2], norm_bias[2])
        .astype(jnp.bfloat16)
        .reshape(rows * cols, width)
    )
    expanded = jnp.dot(tnorm, up_weight, preferred_element_type=jnp.float32)
    act = (jax.nn.silu(expanded[:, :inner]) * expanded[:, inner:]).astype(jnp.bfloat16)
    back = jnp.dot(act, down_weight, preferred_element_type=jnp.float32).reshape(rows, cols, width)
    return (field + back).astype(jnp.bfloat16)


def solution(mesh):
    placed = (P("row", "col", None), P(), P(), P(), P(), P(), P(), P(), P())
    return jax.shard_map(
        body, mesh=mesh, in_specs=placed, out_specs=P("row", "col", None), check_vma=False
    )
```

profile of v0, /device:TPU:2, one launch (start us, length us, event | category | flops | bytes accessed | tf_op | source)
XLA Modules:
  0.0 745.6 jit_solution(11462558896871270672)
XLA Ops:
  6.5 1.2 convert_reduce_fusion
  7.8 1.3 fusion.7
  9.1 0.8 slice_bitcast_fusion
  9.9 1.6 fusion.34
  11.5 1.1 fusion.22
  12.7 0.7 all-gather.7.cloned.1.call-update
  13.4 100.8 %all-gather.5.cloned.1.call-done = bf16[32,512,128]{2,1,0:T(8,128)(2,1)} async-done(((bf16[32,32,128]{2,1,0:T(8,128)(2,1)}), bf16[32,512,128]{2,1,0:T(8,128)(2,1)}) %all-gather.5.cloned.1.call-update) | async-done | bytes 4194320 | tf_op jit(solution)/shard_map/all_gather | solution.py:48
  114.2 2.2 broadcast_select_fusion.1
  116.5 0.6 copy-done.4
  117.1 98.1 %all-gather.7.cloned.1.call-done = bf16[32,512,128]{2,1,0:T(8,128)(2,1)} async-done(((bf16[32,32,128]{2,1,0:T(8,128)(2,1)}), bf16[32,512,128]{2,1,0:T(8,128)(2,1)}) %all-gather.7.cloned.1.call-update) | async-done | bytes 4194320 | tf_op jit(solution)/shard_map/all_gather | solution.py:47
  215.2 7.9 %copy.47 = bf16[32,512,128]{1,0,2:T(8,128)(2,1)} copy(bf16[32,512,128]{2,1,0:T(8,128)(2,1)} %all-gather.7.cloned.1.call-done) | data formatting | bytes 8388608 | tf_op jit(solution)/shard_map/all_gather | solution.py:47
  223.2 156.7 %all-reduce.3.cloned.1.call-done = bf16[32,512,128]{2,1,0:T(8,128)(2,1)} async-done(((bf16[32,512,128]{2,1,0:T(8,128)(2,1)}), bf16[32,512,128]{2,1,0:T(8,128)(2,1)}) %all-reduce.3.cloned.1.call-update) | async-done | bytes 4194320 | tf_op jit(solution)/shard_map/psum | solution.py:9
  379.9 8.0 %copy.46 = bf16[32,512,128]{1,0,2:T(8,128)(2,1)} copy(bf16[32,512,128]{2,1,0:T(8,128)(2,1)} %all-reduce.3.cloned.1.call-done) | data formatting | bytes 8388608 | tf_op jit(solution)/shard_map/psum | solution.py:9
  387.8 6.1 bitcast_reduce_fusion.1
  394.0 3.6 copy.48
  397.7 1.4 multiply_reduce_fusion.3
  399.1 1.6 fusion.61
  401.5 0.6 fusion.33
  402.1 1.1 fusion.11
  403.3 0.5 all-gather.9.cloned.1.call-update
  404.1 58.9 %all-gather.11.cloned.1.call-done = bf16[512,32,128]{2,1,0:T(8,128)(2,1)} async-done(((bf16[32,32,128]{2,1,0:T(8,128)(2,1)}), bf16[512,32,128]{2,1,0:T(8,128)(2,1)}) %all-gather.11.cloned.1.call-update) | async-done | bytes 4194320 | tf_op jit(solution)/shard_map/all_gather | solution.py:56
  462.9 8.6 %copy.53 = bf16[512,32,128]{0,1,2:T(8,128)(2,1)} copy(bf16[512,32,128]{2,1,0:T(8,128)(2,1)} %all-gather.11.cloned.1.call-done) | data formatting | bytes 8388608 | tf_op jit(solution)/shard_map/all_gather | solution.py:56
  471.5 2.2 broadcast_select_fusion
  473.8 50.0 %all-gather.9.cloned.1.call-done = bf16[512,32,128]{2,1,0:T(8,128)(2,1)} async-done(((bf16[32,32,128]{2,1,0:T(8,128)(2,1)}), bf16[512,32,128]{2,1,0:T(8,128)(2,1)}) %all-gather.9.cloned.1.call-update) | async-done | bytes 4194320 | tf_op jit(solution)/shard_map/all_gather | solution.py:57
  523.8 8.5 %copy.54 = bf16[512,32,128]{0,1,2:T(8,128)(2,1)} copy(bf16[512,32,128]{2,1,0:T(8,128)(2,1)} %all-gather.9.cloned.1.call-done) | data formatting | bytes 8388608 | tf_op jit(solution)/shard_map/all_gather | solution.py:57
  532.4 192.4 %all-reduce.5.cloned.1.call-done = bf16[512,32,128]{0,1,2:T(8,128)(2,1)} async-done(((bf16[512,32,128]{0,1,2:T(8,128)(2,1)}), bf16[512,32,128]{0,1,2:T(8,128)(2,1)}) %all-reduce.5.cloned.1.call-update) | async-done | bytes 4194320 | tf_op jit(solution)/shard_map/psum | solution.py:9
  724.7 6.0 bitcast_reduce_fusion
  730.9 2.8 copy.55
  734.1 1.6 fusion.62
  736.5 0.7 fusion.63
  737.2 0.7 fusion.3
  737.9 0.8 add_convert_fusion
  (42 shorter events, 2.6 us)
Async XLA Ops:
  6.5 730.0 %copy-start = (bf16[128,1024]{1,0:T(8,128)(2,1)S(1)}, bf16[128,1024]{1,0:T(8,128)(2,1)}, u32[]{:S(2)}) copy-start(bf16[128,1024]{1,0:T(8,128)(2,1)} %param.16) | copy-start | bytes 786436
  6.5 107.7 %all-gather.5.cloned.1.call-start = ((), (), s32[]{:S(2)}) async-start(), calls=%async_computation | async-start | bytes 4456448 | tf_op jit(solution)/shard_map/all_gather | solution.py:48
  12.6 202.6 %all-gather.7.cloned.1.call-start = ((), (), s32[]{:S(2)}) async-start(), calls=%async_computation.2 | async-start | bytes 4456448 | tf_op jit(solution)/shard_map/all_gather | solution.py:47
  13.4 366.5 %all-reduce.3.cloned.1.call-start = ((), (), s32[]{:S(2)}) async-start(), calls=%async_computation.1 | async-start | bytes 8388608 | tf_op jit(solution)/shard_map/psum | solution.py:9
  116.4 0.7 copy-start.4
  116.4 0.7 copy-start.5
  116.5 346.5 %all-gather.11.cloned.1.call-start = ((), (), s32[]{:S(2)}) async-start(), calls=%async_computation.4 | async-start | bytes 4456448 | tf_op jit(solution)/shard_map/all_gather | solution.py:56
  387.8 11.3 %copy-start.1 = (bf16[32,32,128]{2,1,0:T(8,128)(2,1)S(1)}, bf16[32,32,128]{2,1,0:T(8,128)(2,1)}, u32[]{:S(2)}) copy-start(bf16[32,32,128]{2,1,0:T(8,128)(2,1)} %param.9) | copy-start | bytes 786436
  394.0 7.5 %copy-start.3 = (bf16[2,128,640]{2,1,0:T(8,128)(2,1)S(1)}, bf16[2,128,640]{2,1,0:T(8,128)(2,1)}, u32[]{:S(2)}) copy-start(bf16[2,128,640]{2,1,0:T(8,128)(2,1)} %param.12) | copy-start | bytes 983044
  400.7 0.8 copy-start.2
  403.2 120.6 %all-gather.9.cloned.1.call-start = ((), (), s32[]{:S(2)}) async-start(), calls=%async_computation.3 | async-start | bytes 4456448 | tf_op jit(solution)/shard_map/all_gather | solution.py:57
  403.8 320.9 %all-reduce.5.cloned.1.call-start = ((), (), s32[]{:S(2)}) async-start(), calls=%async_computation.5 | async-start | bytes 8388608 | tf_op jit(solution)/shard_map/psum | solution.py:9
  532.4 201.7 %copy-start.7 = (bf16[2,128,128]{2,1,0:T(8,128)(2,1)S(1)}, bf16[2,128,128]{2,1,0:T(8,128)(2,1)}, u32[]{:S(2)}) copy-start(bf16[2,128,128]{2,1,0:T(8,128)(2,1)} %param.15) | copy-start | bytes 196612
  734.1 3.1 copy-start.6
Sparse Core Ops, SparseCore 0:
  12.7 101.4 all-gather.4
  116.0 99.1 all-gather.6
  217.9 161.9 all-reduce.2
  403.3 59.5 all-gather.10
  465.5 58.2 all-gather.8
  526.3 198.3 all-reduce.4
where the time goes:
time: 747 us; the launch traced here: 746 us
  waiting for transfers between devices  658 us (88%)
  local copies, waits for them, and re-layouts  41.5 us (6%)
  matrix products  19 us (3%)
  between operations  13.7 us (2%)
  other arithmetic  12.9 us (2%)
    psum x2, waiting for transfers between devices, spread(): return lax.psum(kept, axis)  349 us
    all_gather x1, waiting for transfers between devices, body(): lax.all_gather(right, 'col', axis=1, tiled=True)  101 us
    all_gather x1, waiting for transfers between devices, body(): lax.all_gather(left, 'col', axis=1, tiled=True)  98.1 us
    all_gather x1, waiting for transfers between devices, body(): lax.all_gather(left, 'row', axis=0, tiled=True)  58.9 us
    all_gather x1, waiting for transfers between devices, body(): lax.all_gather(right, 'row', axis=0, tiled=True)  50 us
  transfers between devices with their start and end apart: 6, of which 6 were waited for; matrix products, arithmetic and copies ran while one was open for 4% of the time, Pallas kernels for 0%

commit v1 on v0

v1 whole, which is shorter than its diff:
```python
import jax
import jax.numpy as jnp
from jax import lax
from jax.experimental import pallas as pl
from jax.experimental.pallas import tpu as pltpu
from jax.sharding import PartitionSpec as P

F32 = jnp.float32
BF16 = jnp.bfloat16
WIDTH = 128
SIDE = 32
STEPS = 8
FOLD = 4
PAIRS = 8
COLS = 16
CHUNK = 2

PARITY = [[(2 * a + core) * COLS + q for a in range(PAIRS) for q in range(COLS)] for core in (0, 1)]


def exchange(values):
    return lax.all_to_all(values, ("row", "col"), 0, 0, axis_index_groups=PARITY)


def swap_cores(values):
    return lax.ppermute(values, "row", [(i, i ^ 1) for i in range(2 * PAIRS)])


def column(ref, which):
    return jnp.broadcast_to(ref[which : which + 1, :], (WIDTH, WIDTH)).T[:, :1]


def layer_norm(values, gain, bias):
    mean = jnp.mean(values, axis=0, keepdims=True)
    centred = values - mean
    var = jnp.mean(centred * centred, axis=0, keepdims=True)
    return centred * lax.rsqrt(var + 1e-05) * gain + bias


def dot(a, b):
    return lax.dot_general(a, b, (((1,), (0,)), ((), ())), preferred_element_type=F32)


def prepare(field, gain, bias, weight):
    normed = layer_norm(field, gain, bias).astype(BF16)
    proj = dot(weight, normed)
    h = WIDTH
    left = jax.nn.sigmoid(proj[:h]) * proj[h : 2 * h]
    right = jax.nn.sigmoid(proj[2 * h : 3 * h]) * proj[3 * h : 4 * h]
    gate = jax.nn.sigmoid(proj[4 * h :])
    return left, right, gate


def finish(field, mixed, gain, bias, weight, gate):
    mixnorm = layer_norm(mixed, gain, bias).astype(BF16)
    return field + gate * dot(weight, mixnorm)


def put_factors(scratch, chunk, left, right):
    for i in range(CHUNK):
        step = chunk * CHUNK + i
        lanes = slice(i * 128, (i + 1) * 128)
        scratch[pl.ds(step, WIDTH, stride=2 * STEPS), :] = left[:, lanes]
        scratch[pl.ds(step + STEPS, WIDTH, stride=2 * STEPS), :] = right[:, lanes]


def take_mixed(scratch, chunk):
    parts = [
        scratch[pl.ds(chunk * CHUNK + i, WIDTH, stride=STEPS), :] for i in range(CHUNK)
    ]
    return jnp.concatenate(parts, axis=1)


def lanes_of(chunk):
    return slice(chunk * CHUNK * 128, (chunk + 1) * CHUNK * 128)


def first_kernel(pair, norm_gain, norm_bias, weight, factors, gates, fields, scratch):
    gain, bias = column(norm_gain, 0), column(norm_bias, 0)
    weight = weight[0].T
    for chunk in range(STEPS // CHUNK):
        parts = []
        for i in range(CHUNK):
            block = pair[:, chunk * CHUNK + i].astype(F32)
            parts.append(block.reshape(FOLD * SIDE, WIDTH).T)
        field = jnp.concatenate(parts, axis=1)
        left, right, gate = prepare(field, gain, bias, weight)
        put_factors(scratch, chunk, left, right)
        gates[:, lanes_of(chunk)] = gate
        fields[:, lanes_of(chunk)] = field
    factors[...] = scratch[...].reshape(WIDTH, 2 * STEPS, 128).astype(BF16)


def middle_kernel(
    mixed, gates, fields, norm_gain, norm_bias, weight, out_gain, out_bias, out_weight,
    factors, gates_out, fields_out, scratch, product,
):
    gain, bias = column(norm_gain, 1), column(norm_bias, 1)
    mix_gain, mix_bias = column(out_gain, 0), column(out_bias, 0)
    weight = weight[1].T
    out_w = out_weight[0].T
    product[...] = mixed[...].astype(F32).reshape(WIDTH * STEPS, 128)
    for chunk in range(STEPS // CHUNK):
        lanes = lanes_of(chunk)
        field = finish(
            fields[:, lanes], take_mixed(product, chunk), mix_gain, mix_bias, out_w, gates[:, lanes]
        )
        left, right, gate = prepare(field, gain, bias, weight)
        put_factors(scratch, chunk, left, right)
        gates_out[:, lanes] = gate
        fields_out[:, lanes] = field
    factors[...] = scratch[...].reshape(WIDTH, 2 * STEPS, 128).astype(BF16)


def last_kernel(
    mixed, gates, fields, norm_gain, norm_bias, out_gain, out_bias, out_weight, up, down,
    updated, product,
):
    gain, bias = column(norm_gain, 2), column(norm_bias, 2)
    mix_gain, mix_bias = column(out_gain, 1), column(out_bias, 1)
    out_w = out_weight[1].T
    up_w = up[...].T
    down_w = down[...].T
    inner = down.shape[0]
    product[...] = mixed[...].astype(F32).reshape(WIDTH * STEPS, 128)
    for chunk in range(STEPS // CHUNK):
        lanes = lanes_of(chunk)
        field = finish(
            fields[:, lanes], take_mixed(product, chunk), mix_gain, mix_bias, out_w, gates[:, lanes]
        )
        tnorm = layer_norm(field, gain, bias).astype(BF16)
        expanded = dot(up_w, tnorm)
        act = (jax.nn.silu(expanded[:inner]) * expanded[inner:]).astype(BF16)
        field = field + dot(down_w, act)
        for i in range(CHUNK):
            block = field[:, i * 128 : (i + 1) * 128].T.reshape(FOLD, SIDE, WIDTH)
            updated[:, chunk * CHUNK + i] = block.astype(BF16)


def turn(tiles):
    lane = lax.broadcasted_iota(jnp.int32, tiles[0].shape, 1)
    low = lane < 64
    even = (lane & 32) == 0
    a, b, c, d = tiles
    a, c = jnp.where(low, a, pltpu.roll(c, 64, 1)), jnp.where(low, pltpu.roll(a, 64, 1), c)
    b, d = jnp.where(low, b, pltpu.roll(d, 64, 1)), jnp.where(low, pltpu.roll(b, 64, 1), d)
    a, b = jnp.where(even, a, pltpu.roll(b, 32, 1)), jnp.where(even, pltpu.roll(a, 96, 1), b)
    c, d = jnp.where(even, c, pltpu.roll(d, 32, 1)), jnp.where(even, pltpu.roll(c, 96, 1), d)
    return a, b, c, d


def rows_of(tiles):
    return jnp.concatenate(turn(tiles), axis=0).astype(BF16)


def send_product(mixed, product):
    for a in range(PAIRS):
        for g in range(COLS // FOLD):
            tiles = [
                mixed[a * SIDE + i * STEPS : a * SIDE + (i + 1) * STEPS, g * 128 : (g + 1) * 128]
                for i in range(FOLD)
            ]
            for i, tile in enumerate(turn(tiles)):
                product[a * COLS + g * FOLD + i] = tile.astype(BF16)


def outgoing_kernel(own, other, product, left, right):
    core = lax.rem(lax.axis_index("row"), 2)

    def form(a, _):
        for g in range(COLS // FOLD):
            lanes = slice(g * 128, (g + 1) * 128)
            mine = [own[a * COLS + g * FOLD + i].astype(F32) for i in range(FOLD)]
            left[pl.ds(a * SIDE, SIDE), lanes] = rows_of([t[:STEPS] for t in mine])
            row = pl.multiple_of((2 * a + core) * SIDE, SIDE)
            right[pl.ds(row, SIDE), lanes] = rows_of([t[STEPS:] for t in mine])
            theirs = [other[a * COLS + g * FOLD + i].astype(F32) for i in range(FOLD)]
            row = pl.multiple_of((2 * a + 1 - core) * SIDE, SIDE)
            right[pl.ds(row, SIDE), lanes] = rows_of([t[STEPS:] for t in theirs])
        return 0

    lax.fori_loop(0, PAIRS, form, 0)
    mixed = lax.dot_general(
        left[...], right[...], (((1,), (1,)), ((), ())), preferred_element_type=F32
    )
    send_product(mixed, product)


def incoming_kernel(own, other, product, left, right):
    core = lax.rem(lax.axis_index("row"), 2)

    def form(a, _):
        for part, source in enumerate((own, other)):
            row = pl.ds(part * PAIRS * SIDE + a * SIDE, SIDE)
            for g in range(COLS // FOLD):
                tiles = [source[a * COLS + g * FOLD + i].astype(F32) for i in range(FOLD)]
                right[row, g * 128 : (g + 1) * 128] = rows_of([t[STEPS:] for t in tiles])
            for g in range(COLS // FOLD // 2):
                tiles = [
                    source[a * COLS + 2 * (g * FOLD + i) + core].astype(F32) for i in range(FOLD)
                ]
                left[row, g * 128 : (g + 1) * 128] = rows_of([t[:STEPS] for t in tiles])
        return 0

    lax.fori_loop(0, PAIRS, form, 0)
    mixed = lax.dot_general(
        left[...], right[...], (((0,), (0,)), ((), ())), preferred_element_type=F32
    )
    send_product(mixed, product)


def call(kernel, outs, scratch, name):
    return pl.pallas_call(
        kernel,
        out_shape=outs,
        scratch_shapes=scratch,
        compiler_params=pltpu.CompilerParams(vmem_limit_bytes=40 * 1024 * 1024),
        name=name,
    )


def multiply(kernel, factors, shapes, name):
    other = swap_cores(factors)
    product = jax.ShapeDtypeStruct((WIDTH, STEPS, 128), BF16)
    scratch = [pltpu.VMEM(shape, BF16) for shape in shapes]
    return call(kernel, product, scratch, name)(factors, other)


def body(
    pair, norm_gain, norm_bias, proj_weight, out_gain, out_bias, out_weight, up_weight, down_weight
):
    flat = jax.ShapeDtypeStruct((WIDTH, STEPS * 128), F32)
    packed = jax.ShapeDtypeStruct((WIDTH, 2 * STEPS, 128), BF16)
    packing = pltpu.VMEM((WIDTH * 2 * STEPS, 128), F32)
    unpacking = pltpu.VMEM((WIDTH * STEPS, 128), F32)
    size = PAIRS * SIDE

    factors, gate, field = call(first_kernel, (packed, flat, flat), [packing], "first")(
        pair.reshape(FOLD, STEPS, SIDE, WIDTH), norm_gain, norm_bias, proj_weight
    )
    factors = exchange(factors)
    shapes = ((size, 2 * size), (2 * size, 2 * size))
    mixed = exchange(multiply(outgoing_kernel, factors, shapes, "outgoing"))
    factors, gate, field = call(
        middle_kernel, (packed, flat, flat), [packing, unpacking], "middle"
    )(mixed, gate, field, norm_gain, norm_bias, proj_weight, out_gain, out_bias, out_weight)
    factors = exchange(factors)
    shapes = ((2 * size, size), (2 * size, 2 * size))
    mixed = exchange(multiply(incoming_kernel, factors, shapes, "incoming"))
    out = jax.ShapeDtypeStruct((FOLD, STEPS, SIDE, WIDTH), BF16)
    updated = call(last_kernel, out, [unpacking], "last")(
        mixed, gate, field, norm_gain, norm_bias, out_gain, out_bias, out_weight,
        up_weight, down_weight,
    )
    return updated.reshape(FOLD * STEPS, SIDE, WIDTH)


def solution(mesh):
    placed = (P("row", "col", None), P(), P(), P(), P(), P(), P(), P(), P())
    return jax.shard_map(
        body, mesh=mesh, in_specs=placed, out_specs=P("row", "col", None), check_vma=False
    )
```

time: 747 us -> 121 us (0.16)
  waiting for transfers between devices: 658 us -> 3.81 us
  blocking collectives: 0 us -> 103 us
  local copies, waits for them, and re-layouts: 41.5 us -> 3.99 us
  matrix products: 19 us -> 0 us
  between operations: 13.7 us -> 0.11 us
  other arithmetic: 12.9 us -> 0 us
  Pallas kernels: 0 us -> 9.56 us
    psum x2 -> x0, waiting for transfers between devices: 349 us -> none  [spread(): return lax.psum(kept, axis)]
    all_gather x4 -> x0, waiting for transfers between devices: 308 us -> none  [the longest x1 101 us: body(): lax.all_gather(right, 'col', axis=1, tiled=True)]
    all_to_all x0 -> x4, blocking collectives: none -> 103 us  [exchange(): lax.all_to_all(values, ('row', 'col'), 0, 0, axis_index_groups=PARITY)]
    all_gather x3 -> x0, local copies, waits for them, and re-layouts: 25.1 us -> none  [the longest x1 8.6 us: body(): lax.all_gather(left, 'row', axis=0, tiled=True)]
    dot_general x8 -> x0, matrix products: 19 us -> none  [the longest x1 6.13 us: body(): jnp.einsum('ikc,jkc->ijc', left_rows, pieces, preferred_element_type=jnp....]
    pallas_call x0 -> x5, Pallas kernels: none -> 9.56 us  [the longest x2 3.7 us: multiply(): return call(kernel, product, scratch, name)(factors, other)]
    psum x1 -> x0, local copies, waits for them, and re-layouts: 7.99 us -> none  [spread(): return lax.psum(kept, axis)]
  transfers between devices with their start and end apart: 6 -> 2, of which waited for: 6 -> 2; matrix products, arithmetic and copies ran while one was open for 4% -> 0% of each run, Pallas kernels for 0% -> 0%
where the time goes in v1:
time: 121 us; the launch traced here: 120 us
  blocking collectives  103 us (85%)
  Pallas kernels  9.56 us (8%)
  local copies, waits for them, and re-layouts  3.99 us (3%)
  waiting for transfers between devices  3.81 us (3%)
    all_to_all x4, blocking collectives, exchange(): lax.all_to_all(values, ('row', 'col'), 0, 0, axis_index_groups=PARITY)  103 us
    unnamed x24, local copies, waits for them, and re-layouts  3.99 us
    ppermute x2, waiting for transfers between devices, swap_cores(): return lax.ppermute(values, 'row', [(i, i ^ 1) for i in range(2 * PAIRS)])  3.81 us
    pallas_call x2, Pallas kernels, multiply(): return call(kernel, product, scratch, name)(factors, other)  3.7 us
    pallas_call x1, Pallas kernels, body(): call(last_kernel, out, [unpacking], 'last')  3.62 us
  transfers between devices with their start and end apart: 2, of which 2 were waited for; matrix products, arithmetic and copies ran while one was open for 0% of the time, Pallas kernels for 0%

profile of v1, /device:TPU:2, one launch (start us, length us, event | category | flops | bytes accessed | tf_op | source)
XLA Modules:
  0.0 120.3 jit_solution(16181107082616836957)
XLA Ops:
  0.0 0.0 copy-start
  0.0 1.0 copy-done
  1.0 0.9 copy-done.3
  1.9 0.7 copy-done.6
  2.6 0.7 copy-done.8
  3.3 0.9 first.1
  4.2 34.7 %all_to_all.20.own = bf16[128,16,128]{2,1,0:T(8,128)(2,1)S(1)} all-to-all(bf16[128,16,128]{2,1,0:T(8,128)(2,1)S(1)} %get-tuple-element.11), channel_id=1, replica_groups={{0,1,2,3,4,5,6,7,8,9,10,11,12,13,14,15,32,33,34,35,36,37,38,39,40,41,42..., dimensions={0} | all-to-all | bytes 1048576 | tf_op jit(solution)/shard_map/all_to_all | solution.py:22
  38.9 0.0 collective-permute-start
  38.9 1.9 %collective-permute-done.other = bf16[128,16,128]{2,1,0:T(8,128)(2,1)S(1)} collective-permute-done((bf16[128,16,128]{2,1,0:T(8,128)(2,1)S(1)}, bf16[128,16,128]{2,1,0:T(8,128)(2,1)S(1)}, u32[]{:S(2)}, u32[]{:S(2)}) %collective-permute-start) | collective-permute-done | bytes 524320 | tf_op jit(solution)/shard_map/ppermute | solution.py:26
  40.8 1.9 %outgoing.1 = bf16[128,8,128]{2,1,0:T(8,128)(2,1)S(1)} custom-call(bf16[128,16,128]{2,1,0:T(8,128)(2,1)S(1)} %all_to_all.20.own, bf16[128,16,128]{2,1,0:T(8,128)(2,1)S(1)} %collective-permute-done.other), custom_call_target="tpu_custom_call" | custom-call | tf_op jit(solution)/shard_map/outgoing/pallas_call | solution.py:226
  42.6 0.0 copy-start.1
  42.7 0.0 copy-start.4
  42.7 0.0 copy-start.9
  42.7 0.0 copy-start.11
  42.7 21.4 %all_to_all.21.mixed = bf16[128,8,128]{2,1,0:T(8,128)(2,1)S(1)} all-to-all(bf16[128,8,128]{2,1,0:T(8,128)(2,1)S(1)} %outgoing.1), channel_id=1, replica_groups={{0,1,2,3,4,5,6,7,8,9,10,11,12,13,14,15,32,33,34,35,36,37,38,39,40,41,42..., dimensions={0} | all-to-all | bytes 524288 | tf_op jit(solution)/shard_map/all_to_all | solution.py:22
  64.1 0.0 copy-done.1
  64.1 0.0 copy-done.4
  64.1 0.0 copy-done.9
  64.1 0.0 copy-done.11
  64.1 0.6 copy-done.7
  64.8 0.0 copy-done.10
  64.8 1.3 %middle.1 = (bf16[128,16,128]{2,1,0:T(8,128)(2,1)S(1)}, f32[128,1024]{1,0:T(8,128)S(1)}, f32[128,1024]{1,0:T(8,128)S(1)}) custom-call(bf16[128,8,128]{2,1,0:T(8,128)(2,1)S(1)} %all_to_all.21.mixed, f32[128,1024]{1,0:T(8,128)S(1)} %get-tuple-element.12.gates, f32[128,1024]{1,0:T(8,128)S(1)} %get-tuple-element.13.fields, f32[3,128]{1,0:T(4,128)S(1)} %copy-done.7, ...), custom_call_target="tpu_custom_call" | custom-call | tf_op jit(solution)/shard_map/middle/pallas_call | solution.py:244
  66.1 25.3 %all_to_all.22.own = bf16[128,16,128]{2,1,0:T(8,128)(2,1)S(1)} all-to-all(bf16[128,16,128]{2,1,0:T(8,128)(2,1)S(1)} %get-tuple-element.14), channel_id=1, replica_groups={{0,1,2,3,4,5,6,7,8,9,10,11,12,13,14,15,32,33,34,35,36,37,38,39,40,41,42..., dimensions={0} | all-to-all | bytes 1048576 | tf_op jit(solution)/shard_map/all_to_all | solution.py:22
  91.5 0.0 collective-permute-start.1
  91.5 1.9 %collective-permute-done.1.other = bf16[128,16,128]{2,1,0:T(8,128)(2,1)S(1)} collective-permute-done((bf16[128,16,128]{2,1,0:T(8,128)(2,1)S(1)}, bf16[128,16,128]{2,1,0:T(8,128)(2,1)S(1)}, u32[]{:S(2)}, u32[]{:S(2)}) %collective-permute-start.1) | collective-permute-done | bytes 524320 | tf_op jit(solution)/shard_map/ppermute | solution.py:26
  93.4 1.9 %incoming.1 = bf16[128,8,128]{2,1,0:T(8,128)(2,1)S(1)} custom-call(bf16[128,16,128]{2,1,0:T(8,128)(2,1)S(1)} %all_to_all.22.own, bf16[128,16,128]{2,1,0:T(8,128)(2,1)S(1)} %collective-permute-done.1.other), custom_call_target="tpu_custom_call" | custom-call | tf_op jit(solution)/shard_map/incoming/pallas_call | solution.py:226
  95.2 0.0 copy-start.2
  95.2 0.0 copy-start.5
  95.2 21.4 %all_to_all.23.mixed = bf16[128,8,128]{2,1,0:T(8,128)(2,1)S(1)} all-to-all(bf16[128,8,128]{2,1,0:T(8,128)(2,1)S(1)} %incoming.1), channel_id=1, replica_groups={{0,1,2,3,4,5,6,7,8,9,10,11,12,13,14,15,32,33,34,35,36,37,38,39,40,41,42..., dimensions={0} | all-to-all | bytes 524288 | tf_op jit(solution)/shard_map/all_to_all | solution.py:22
  116.7 0.0 copy-done.2
  116.7 0.0 copy-done.5
  116.7 3.6 %last.1 = bf16[4,8,32,128]{3,2,1,0:T(8,128)(2,1)} custom-call(bf16[128,8,128]{2,1,0:T(8,128)(2,1)S(1)} %all_to_all.23.mixed, f32[128,1024]{1,0:T(8,128)S(1)} %get-tuple-element.15.gates, f32[128,1024]{1,0:T(8,128)S(1)} %get-tuple-element.16.fields, f32[3,128]{1,0:T(4,128)S(1)} %copy-done.7, f32[3,128]{1,0:T(4,128)S(1)} %copy-done.9, ...), custom_call_target="tpu_custom_call" | custom-call | tf_op jit(solution)/shard_map/last/pallas_call | solution.py:251
  (5 shorter events, 0.0 us)
Async XLA Ops:
  0.0 1.0 copy-start
  1.0 0.9 copy-start.3
  1.9 0.7 copy-start.6
  2.6 0.7 copy-start.8
  38.9 1.9 %collective-permute-start = (bf16[128,16,128]{2,1,0:T(8,128)(2,1)S(1)}, bf16[128,16,128]{2,1,0:T(8,128)(2,1)S(1)}, u32[]{:S(2)}, u32[]{:S(2)}) collective-permute-start(bf16[128,16,128]{2,1,0:T(8,128)(2,1)S(1)} %all_to_all.20.own), channel_id=1, source_target_pairs={{0,16},{16,0},{32,48},{48,32},{64,80},{80,64},{96,112},{112,96},{1... | collective-permute-start | bytes 1572872 | tf_op jit(solution)/shard_map/ppermute | solution.py:26
  42.6 21.5 %copy-start.1 = (bf16[2,128,640]{2,1,0:T(8,128)(2,1)S(1)}, bf16[2,128,640]{2,1,0:T(8,128)(2,1)}, u32[]{:S(2)}) copy-start(bf16[2,128,640]{2,1,0:T(8,128)(2,1)} %weight.3) | copy-start | bytes 983044
  42.7 21.5 %copy-start.4 = (bf16[2,128,128]{2,1,0:T(8,128)(2,1)S(1)}, bf16[2,128,128]{2,1,0:T(8,128)(2,1)}, u32[]{:S(2)}) copy-start(bf16[2,128,128]{2,1,0:T(8,128)(2,1)} %out_weight.3) | copy-start | bytes 196612
  42.7 21.4 %copy-start.9 = (f32[3,128]{1,0:T(4,128)S(1)}, f32[3,128]{1,0:T(4,128)}, u32[]{:S(2)}) copy-start(f32[3,128]{1,0:T(4,128)} %norm_bias.5) | copy-start | bytes 4612
  42.7 21.4 %copy-start.11 = (f32[2,128]{1,0:T(2,128)S(1)}, f32[2,128]{1,0:T(2,128)}, u32[]{:S(2)}) copy-start(f32[2,128]{1,0:T(2,128)} %out_bias.3) | copy-start | bytes 3076
  64.1 0.7 copy-start.7
  64.1 0.7 copy-start.10
  91.5 1.9 %collective-permute-start.1 = (bf16[128,16,128]{2,1,0:T(8,128)(2,1)S(1)}, bf16[128,16,128]{2,1,0:T(8,128)(2,1)S(1)}, u32[]{:S(2)}, u32[]{:S(2)}) collective-permute-start(bf16[128,16,128]{2,1,0:T(8,128)(2,1)S(1)} %all_to_all.22.own), channel_id=1, source_target_pairs={{0,16},{16,0},{32,48},{48,32},{64,80},{80,64},{96,112},{112,96},{1... | collective-permute-start | bytes 1572872 | tf_op jit(solution)/shard_map/ppermute | solution.py:26
  95.2 21.4 %copy-start.2 = (bf16[128,1024]{1,0:T(8,128)(2,1)S(1)}, bf16[128,1024]{1,0:T(8,128)(2,1)}, u32[]{:S(2)}) copy-start(bf16[128,1024]{1,0:T(8,128)(2,1)} %up.1) | copy-start | bytes 786436
  95.2 21.4 %copy-start.5 = (bf16[512,128]{1,0:T(8,128)(2,1)S(1)}, bf16[512,128]{1,0:T(8,128)(2,1)}, u32[]{:S(2)}) copy-start(bf16[512,128]{1,0:T(8,128)(2,1)} %down.1) | copy-start | bytes 393220

commit v2 on v1

v2 whole, which is shorter than its diff:
```python
import jax
import jax.numpy as jnp
from jax import lax
from jax.experimental import pallas as pl
from jax.experimental.pallas import tpu as pltpu
from jax.sharding import PartitionSpec as P

F32 = jnp.float32
BF16 = jnp.bfloat16
WIDTH = 128
SIDE = 32
STEPS = 8
FOLD = 4
PAIRS = 8
COLS = 16
HALF = PAIRS * SIDE
FULL = 2 * HALF
CHUNK = 8

PARITY = [[(2 * a + core) * COLS + q for q in range(COLS) for a in range(PAIRS)] for core in (0, 1)]


def member(a, q):
    return q * PAIRS + a


def exchange(values):
    return lax.all_to_all(values, ("row", "col"), 0, 0, axis_index_groups=PARITY)


def swap_cores(values):
    return lax.ppermute(values, "row", [(i, i ^ 1) for i in range(2 * PAIRS)])


def core_index():
    return lax.rem(lax.axis_index("row"), 2)


def sigmoid(x):
    return 0.5 + 0.5 * jnp.tanh(0.5 * x)


def layer_norm(values, gain, bias):
    mean = jnp.mean(values, axis=0, keepdims=True)
    centred = values - mean
    var = jnp.mean(centred * centred, axis=0, keepdims=True)
    return centred * lax.rsqrt(var + 1e-05) * gain + bias


def dot(a, b):
    return lax.dot_general(a, b, (((1,), (0,)), ((), ())), preferred_element_type=F32)


def prepare(field, gain, bias, weight):
    normed = layer_norm(field, gain, bias).astype(BF16)
    proj = dot(weight, normed)
    h = WIDTH
    left = sigmoid(proj[:h]) * proj[h : 2 * h]
    right = sigmoid(proj[2 * h : 3 * h]) * proj[3 * h : 4 * h]
    gate = sigmoid(proj[4 * h :])
    return left, right, gate


def finish(field, mixed, gain, bias, weight, gate):
    mixnorm = layer_norm(mixed, gain, bias).astype(BF16)
    return field + gate * dot(weight, mixnorm)


def put_factors(scratch, chunk, left, right):
    for i in range(CHUNK):
        step = chunk * CHUNK + i
        lanes = slice(i * 128, (i + 1) * 128)
        scratch[pl.ds(step, WIDTH, stride=2 * STEPS), :] = left[:, lanes]
        scratch[pl.ds(step + STEPS, WIDTH, stride=2 * STEPS), :] = right[:, lanes]


def take_mixed(scratch, chunk):
    parts = [scratch[pl.ds(chunk * CHUNK + i, WIDTH, stride=STEPS), :] for i in range(CHUNK)]
    return jnp.concatenate(parts, axis=1)


def lanes_of(chunk):
    return slice(chunk * CHUNK * 128, (chunk + 1) * CHUNK * 128)


def first_kernel(
    pair_hbm, norm_gain_hbm, norm_bias_hbm, out_gain_hbm, out_bias_hbm, weight_hbm,
    factors, gates, fields, vectors,
    pair, norm_gain, norm_bias, out_gain, out_bias, weight, scratch, sems,
):
    copies = [
        pltpu.make_async_copy(source, target, sems.at[i])
        for i, (source, target) in enumerate(
            (
                (weight_hbm.at[0], weight),
                (pair_hbm, pair),
                (norm_gain_hbm, norm_gain),
                (norm_bias_hbm, norm_bias),
                (out_gain_hbm, out_gain),
                (out_bias_hbm, out_bias),
            )
        )
    ]
    for copy in copies:
        copy.start()
    for copy in copies:
        copy.wait()
    rows = [norm_gain[...], norm_bias[...], out_gain[...], out_bias[...]]
    rows = jnp.concatenate(rows + [jnp.zeros((WIDTH - 10, WIDTH), F32)], axis=0)
    vectors[...] = rows.T
    gain, bias = vectors[:, 0:1], vectors[:, 3:4]
    weight = weight[...].T
    for chunk in range(STEPS // CHUNK):
        parts = []
        for i in range(CHUNK):
            block = pair[:, chunk * CHUNK + i].astype(F32)
            parts.append(block.reshape(FOLD * SIDE, WIDTH).T)
        field = jnp.concatenate(parts, axis=1)
        left, right, gate = prepare(field, gain, bias, weight)
        put_factors(scratch, chunk, left, right)
        gates[:, lanes_of(chunk)] = gate
        fields[:, lanes_of(chunk)] = field
    factors[...] = scratch[...].reshape(WIDTH, 2 * STEPS, 128).astype(BF16)


def middle_kernel(
    mixed, gates, fields, vectors, weight, out_weight, factors, gates_out, fields_out,
    scratch, product,
):
    gain, bias = vectors[:, 1:2], vectors[:, 4:5]
    mix_gain, mix_bias = vectors[:, 6:7], vectors[:, 8:9]
    proj_w, out_w = weight[1].T, out_weight[0].T
    product[...] = mixed[...].astype(F32).reshape(WIDTH * STEPS, 128)
    for chunk in range(STEPS // CHUNK):
        lanes = lanes_of(chunk)
        field = finish(
            fields[:, lanes], take_mixed(product, chunk), mix_gain, mix_bias,
            out_w, gates[:, lanes],
        )
        left, right, gate = prepare(field, gain, bias, proj_w)
        put_factors(scratch, chunk, left, right)
        gates_out[:, lanes] = gate
        fields_out[:, lanes] = field
    factors[...] = scratch[...].reshape(WIDTH, 2 * STEPS, 128).astype(BF16)


def last_kernel(
    mixed, gates, fields, vectors, out_weight, up, down, updated, product
):
    gain, bias = vectors[:, 2:3], vectors[:, 5:6]
    mix_gain, mix_bias = vectors[:, 7:8], vectors[:, 9:10]
    out_w, up_w, down_w = out_weight[1].T, up[...].T, down[...].T
    inner = down.shape[0]
    product[...] = mixed[...].astype(F32).reshape(WIDTH * STEPS, 128)
    for chunk in range(STEPS // CHUNK):
        lanes = lanes_of(chunk)
        field = finish(
            fields[:, lanes], take_mixed(product, chunk), mix_gain, mix_bias,
            out_w, gates[:, lanes],
        )
        tnorm = layer_norm(field, gain, bias).astype(BF16)
        expanded = dot(up_w, tnorm)
        wide = expanded[:inner]
        act = (wide * sigmoid(wide) * expanded[inner:]).astype(BF16)
        field = field + dot(down_w, act)
        for i in range(CHUNK):
            block = field[:, i * 128 : (i + 1) * 128].T.reshape(FOLD, SIDE, WIDTH)
            updated[:, chunk * CHUNK + i] = block.astype(BF16)


def turn(tiles):
    lane = lax.broadcasted_iota(jnp.int32, tiles[0].shape, 1)
    low = lane < 64
    even = (lane & 32) == 0
    a, b, c, d = tiles
    a, c = jnp.where(low, a, pltpu.roll(c, 64, 1)), jnp.where(low, pltpu.roll(a, 64, 1), c)
    b, d = jnp.where(low, b, pltpu.roll(d, 64, 1)), jnp.where(low, pltpu.roll(b, 64, 1), d)
    a, b = jnp.where(even, a, pltpu.roll(b, 32, 1)), jnp.where(even, pltpu.roll(a, 96, 1), b)
    c, d = jnp.where(even, c, pltpu.roll(d, 32, 1)), jnp.where(even, pltpu.roll(c, 96, 1), d)
    return a, b, c, d


def rows_of(tiles):
    return jnp.concatenate(turn(tiles), axis=0).astype(BF16)


def left_of(source, a, q):
    return source[member(a, q), :STEPS].astype(F32)


def right_of(source, a, q):
    return source[member(a, q), STEPS:].astype(F32)


def lanes_from(g):
    return slice(g * 128, (g + 1) * 128)


def send_product(mixed, product):
    for a in range(PAIRS):
        rows = [slice(a * SIDE + i * STEPS, a * SIDE + (i + 1) * STEPS) for i in range(FOLD)]
        for g in range(COLS // FOLD):
            for i, tile in enumerate(turn([mixed[row, lanes_from(g)] for row in rows])):
                product[member(a, g * FOLD + i)] = tile.astype(BF16)


def outgoing_kernel(own, other, product, left, right):
    core = core_index()

    def form(a, _):
        mine = pl.ds(pl.multiple_of((2 * a + core) * SIDE, SIDE), SIDE)
        theirs = pl.ds(pl.multiple_of((2 * a + 1 - core) * SIDE, SIDE), SIDE)
        for g in range(COLS // FOLD):
            columns = [g * FOLD + i for i in range(FOLD)]
            left[pl.ds(a * SIDE, SIDE), lanes_from(g)] = rows_of(
                [left_of(own, a, q) for q in columns]
            )
            right[mine, lanes_from(g)] = rows_of([right_of(own, a, q) for q in columns])
            right[theirs, lanes_from(g)] = rows_of([right_of(other, a, q) for q in columns])
        return 0

    lax.fori_loop(0, PAIRS, form, 0)
    mixed = lax.dot_general(
        left[...], right[...], (((1,), (1,)), ((), ())), preferred_element_type=F32
    )
    send_product(mixed, product)


def incoming_kernel(own, other, product, left, right):
    core = core_index()

    def form(a, _):
        for part, source in enumerate((own, other)):
            row = pl.ds(part * HALF + a * SIDE, SIDE)
            for g in range(COLS // FOLD):
                columns = [g * FOLD + i for i in range(FOLD)]
                right[row, lanes_from(g)] = rows_of([right_of(source, a, q) for q in columns])
            for g in range(PAIRS // FOLD):
                columns = [2 * (g * FOLD + i) + core for i in range(FOLD)]
                left[row, lanes_from(g)] = rows_of([left_of(source, a, q) for q in columns])
        return 0

    lax.fori_loop(0, PAIRS, form, 0)
    mixed = lax.dot_general(
        left[...], right[...], (((0,), (0,)), ((), ())), preferred_element_type=F32
    )
    send_product(mixed, product)


def call(kernel, outs, scratch, name, vmem=40, **more):
    return pl.pallas_call(
        kernel,
        out_shape=outs,
        scratch_shapes=scratch,
        compiler_params=pltpu.CompilerParams(vmem_limit_bytes=vmem * 1024 * 1024),
        name=name,
        **more,
    )


def shape(*dims, dtype=BF16):
    return jax.ShapeDtypeStruct(dims, dtype)


def body(
    pair, norm_gain, norm_bias, proj_weight, out_gain, out_bias, out_weight, up_weight, down_weight
):
    flat = shape(WIDTH, STEPS * 128, dtype=F32)
    packed = shape(WIDTH, 2 * STEPS, 128)
    product = shape(WIDTH, STEPS, 128)
    packing = pltpu.VMEM((WIDTH * 2 * STEPS, 128), F32)
    unpacking = pltpu.VMEM((WIDTH * STEPS, 128), F32)
    blocks = (FOLD, STEPS, SIDE, WIDTH)

    operands = (pair.reshape(blocks), norm_gain, norm_bias, out_gain, out_bias)
    landing = [pltpu.VMEM(v.shape, v.dtype) for v in operands]
    landing += [pltpu.VMEM(proj_weight.shape[1:], BF16), packing, pltpu.SemaphoreType.DMA((6,))]
    factors, gate, field, vectors = call(
        first_kernel, (packed, flat, flat, shape(WIDTH, WIDTH, dtype=F32)), landing, "first", 60,
        in_specs=[pl.BlockSpec(memory_space=pltpu.HBM)] * 6,
    )(*operands, proj_weight)
    own = exchange(factors)
    left, right = pltpu.VMEM((HALF, FULL), BF16), pltpu.VMEM((FULL, FULL), BF16)
    mixed = call(outgoing_kernel, product, [left, right], "outgoing")(own, swap_cores(own))
    factors, gate, field = call(
        middle_kernel, (packed, flat, flat), [packing, unpacking], "middle"
    )(exchange(mixed), gate, field, vectors, proj_weight, out_weight)
    own = exchange(factors)
    left = pltpu.VMEM((FULL, HALF), BF16)
    mixed = call(incoming_kernel, product, [left, right], "incoming")(own, swap_cores(own))
    updated = call(last_kernel, shape(*blocks), [unpacking], "last")(
        exchange(mixed), gate, field, vectors, out_weight, up_weight, down_weight
    )
    return updated.reshape(FOLD * STEPS, SIDE, WIDTH)


def solution(mesh):
    placed = (P("row", "col", None), P(), P(), P(), P(), P(), P(), P(), P())
    return jax.shard_map(
        body, mesh=mesh, in_specs=placed, out_specs=P("row", "col", None), check_vma=False
    )
```

time: 121 us -> 116 us (0.959)
  local copies, waits for them, and re-layouts: 3.99 us -> 0.04 us
    unnamed x24 -> x14, local copies, waits for them, and re-layouts: 3.99 us -> 0.04 us
where the time goes in v2:
time: 116 us
  blocking collectives  102 us (88%)
  Pallas kernels  10.3 us (9%)
  waiting for transfers between devices  3.81 us (3%)
    all_to_all x4, blocking collectives, exchange(): lax.all_to_all(values, ('row', 'col'), 0, 0, axis_index_groups=PARITY)  102 us
    ppermute x2, waiting for transfers between devices, swap_cores(): return lax.ppermute(values, 'row', [(i, i ^ 1) for i in range(2 * PAIRS)])  3.81 us
    pallas_call x1, Pallas kernels, body(): call(first_kernel, (packed, flat, flat, shape(WIDTH, WIDTH, dtype=F32)),...  3.24 us
  transfers between devices with their start and end apart: 2, of which 2 were waited for; matrix products, arithmetic and copies ran while one was open for 0% of the time, Pallas kernels for 0%

profile of v2, /device:TPU:2, one launch (start us, length us, event | category | flops | bytes accessed | tf_op | source)
XLA Modules:
  0.0 116.0 jit_solution(12563993847620319627)
XLA Ops:
  0.0 3.2 %first.1 = (bf16[128,16,128]{2,1,0:T(8,128)(2,1)}, f32[128,1024]{1,0:T(8,128)}, f32[128,1024]{1,0:T(8,128)}, f32[128,128]{1,0:T(8,128)}) custom-call(bf16[4,8,32,128]{3,2,1,0:T(8,128)(2,1)} %bitcast.2, f32[3,128]{1,0:T(4,128)} %norm_gain_hbm.1, f32[3,128]{1,0:T(4,128)} %norm_bias_hbm.1, f32[2,128]{1,0:T(2,128)} %out_gain_hbm.1, f32[2,128]{1,0:T(2,128)} %out_bias_hbm.1, ...), custom_call_target="tpu_custom_call" | custom-call | tf_op jit(solution)/shard_map/first/pallas_call | solution.py:278
  3.2 34.9 %all_to_all.20.own = bf16[128,16,128]{2,1,0:T(8,128)(2,1)S(1)} all-to-all(bf16[128,16,128]{2,1,0:T(8,128)(2,1)} %get-tuple-element.12), channel_id=1, replica_groups={{0,32,64,96,128,160,192,224,1,33,65,97,129,161,193,225,2,34,66,98,130,1..., dimensions={0} | all-to-all | bytes 1048576 | tf_op jit(solution)/shard_map/all_to_all | solution.py:28
  38.2 0.0 collective-permute-start
  38.2 1.9 %collective-permute-done.other = bf16[128,16,128]{2,1,0:T(8,128)(2,1)S(1)} collective-permute-done((bf16[128,16,128]{2,1,0:T(8,128)(2,1)S(1)}, bf16[128,16,128]{2,1,0:T(8,128)(2,1)S(1)}, u32[]{:S(2)}, u32[]{:S(2)}) %collective-permute-start) | collective-permute-done | bytes 524320 | tf_op jit(solution)/shard_map/ppermute | solution.py:32
  40.1 0.0 copy-start.1
  40.1 0.0 copy-start.2
  40.1 1.9 %outgoing.1 = bf16[128,8,128]{2,1,0:T(8,128)(2,1)S(1)} custom-call(bf16[128,16,128]{2,1,0:T(8,128)(2,1)S(1)} %all_to_all.20.own, bf16[128,16,128]{2,1,0:T(8,128)(2,1)S(1)} %collective-permute-done.other), custom_call_target="tpu_custom_call" | custom-call | tf_op jit(solution)/shard_map/outgoing/pallas_call | solution.py:284
  42.0 0.0 copy-start
  42.0 0.0 copy-start.3
  42.0 0.0 copy-start.4
  42.0 20.8 %all_to_all.21.mixed = bf16[128,8,128]{2,1,0:T(8,128)(2,1)S(1)} all-to-all(bf16[128,8,128]{2,1,0:T(8,128)(2,1)S(1)} %outgoing.1), channel_id=1, replica_groups={{0,32,64,96,128,160,192,224,1,33,65,97,129,161,193,225,2,34,66,98,130,1..., dimensions={0} | all-to-all | bytes 524288 | tf_op jit(solution)/shard_map/all_to_all | solution.py:28
  62.9 0.0 copy-done.1
  62.9 0.0 copy-done.2
  62.9 0.0 copy-done
  62.9 0.0 copy-done.3
  62.9 0.0 copy-done.4
  62.9 1.2 %middle.1 = (bf16[128,16,128]{2,1,0:T(8,128)(2,1)S(1)}, f32[128,1024]{1,0:T(8,128)S(1)}, f32[128,1024]{1,0:T(8,128)S(1)}) custom-call(bf16[128,8,128]{2,1,0:T(8,128)(2,1)S(1)} %all_to_all.21.mixed, f32[128,1024]{1,0:T(8,128)S(1)} %copy-done.1, f32[128,1024]{1,0:T(8,128)S(1)} %copy-done.2, f32[128,128]{1,0:T(8,128)S(1)} %copy-done.4, ...), custom_call_target="tpu_custom_call" | custom-call | tf_op jit(solution)/shard_map/middle/pallas_call | solution.py:285
  64.1 25.1 %all_to_all.22.own = bf16[128,16,128]{2,1,0:T(8,128)(2,1)S(1)} all-to-all(bf16[128,16,128]{2,1,0:T(8,128)(2,1)S(1)} %get-tuple-element.16), channel_id=1, replica_groups={{0,32,64,96,128,160,192,224,1,33,65,97,129,161,193,225,2,34,66,98,130,1..., dimensions={0} | all-to-all | bytes 1048576 | tf_op jit(solution)/shard_map/all_to_all | solution.py:28
  89.2 0.0 collective-permute-start.1
  89.2 1.9 %collective-permute-done.1.other = bf16[128,16,128]{2,1,0:T(8,128)(2,1)S(1)} collective-permute-done((bf16[128,16,128]{2,1,0:T(8,128)(2,1)S(1)}, bf16[128,16,128]{2,1,0:T(8,128)(2,1)S(1)}, u32[]{:S(2)}, u32[]{:S(2)}) %collective-permute-start.1) | collective-permute-done | bytes 524320 | tf_op jit(solution)/shard_map/ppermute | solution.py:32
  91.1 1.9 %incoming.1 = bf16[128,8,128]{2,1,0:T(8,128)(2,1)S(1)} custom-call(bf16[128,16,128]{2,1,0:T(8,128)(2,1)S(1)} %all_to_all.22.own, bf16[128,16,128]{2,1,0:T(8,128)(2,1)S(1)} %collective-permute-done.1.other), custom_call_target="tpu_custom_call" | custom-call | tf_op jit(solution)/shard_map/incoming/pallas_call | solution.py:290
  93.0 0.0 copy-start.5
  93.0 0.0 copy-start.6
  93.0 20.8 %all_to_all.23.mixed = bf16[128,8,128]{2,1,0:T(8,128)(2,1)S(1)} all-to-all(bf16[128,8,128]{2,1,0:T(8,128)(2,1)S(1)} %incoming.1), channel_id=1, replica_groups={{0,32,64,96,128,160,192,224,1,33,65,97,129,161,193,225,2,34,66,98,130,1..., dimensions={0} | all-to-all | bytes 524288 | tf_op jit(solution)/shard_map/all_to_all | solution.py:28
  113.8 0.0 copy-done.5
  113.8 0.0 copy-done.6
  113.8 2.1 %last.1 = bf16[4,8,32,128]{3,2,1,0:T(8,128)(2,1)} custom-call(bf16[128,8,128]{2,1,0:T(8,128)(2,1)S(1)} %all_to_all.23.mixed, f32[128,1024]{1,0:T(8,128)S(1)} %get-tuple-element.17.gates, f32[128,1024]{1,0:T(8,128)S(1)} %get-tuple-element.18.fields, f32[128,128]{1,0:T(8,128)S(1)} %copy-done.4, bf16[2,128,128]{2,1,0:T(8,128)(2,1)S(1)} %copy-done.3, ...), custom_call_target="tpu_custom_call" | custom-call | tf_op jit(solution)/shard_map/last/pallas_call | solution.py:291
Async XLA Ops:
  38.2 1.9 %collective-permute-start = (bf16[128,16,128]{2,1,0:T(8,128)(2,1)S(1)}, bf16[128,16,128]{2,1,0:T(8,128)(2,1)S(1)}, u32[]{:S(2)}, u32[]{:S(2)}) collective-permute-start(bf16[128,16,128]{2,1,0:T(8,128)(2,1)S(1)} %all_to_all.20.own), channel_id=1, source_target_pairs={{0,16},{16,0},{32,48},{48,32},{64,80},{80,64},{96,112},{112,96},{1... | collective-permute-start | bytes 1572872 | tf_op jit(solution)/shard_map/ppermute | solution.py:32
  40.1 22.8 %copy-start.1 = (f32[128,1024]{1,0:T(8,128)S(1)}, f32[128,1024]{1,0:T(8,128)}, u32[]{:S(2)}) copy-start(f32[128,1024]{1,0:T(8,128)} %get-tuple-element.13.gates) | copy-start | bytes 1572868
  40.1 22.8 %copy-start.2 = (f32[128,1024]{1,0:T(8,128)S(1)}, f32[128,1024]{1,0:T(8,128)}, u32[]{:S(2)}) copy-start(f32[128,1024]{1,0:T(8,128)} %get-tuple-element.14.fields) | copy-start | bytes 1572868
  42.0 20.9 %copy-start = (bf16[2,128,640]{2,1,0:T(8,128)(2,1)S(1)}, bf16[2,128,640]{2,1,0:T(8,128)(2,1)}, u32[]{:S(2)}) copy-start(bf16[2,128,640]{2,1,0:T(8,128)(2,1)} %weight.1) | copy-start | bytes 983044
  42.0 20.9 %copy-start.3 = (bf16[2,128,128]{2,1,0:T(8,128)(2,1)S(1)}, bf16[2,128,128]{2,1,0:T(8,128)(2,1)}, u32[]{:S(2)}) copy-start(bf16[2,128,128]{2,1,0:T(8,128)(2,1)} %out_weight.3) | copy-start | bytes 196612
  42.0 20.9 %copy-start.4 = (f32[128,128]{1,0:T(8,128)S(1)}, f32[128,128]{1,0:T(8,128)}, u32[]{:S(2)}) copy-start(f32[128,128]{1,0:T(8,128)} %get-tuple-element.15.vectors) | copy-start | bytes 196612
  89.2 1.9 %collective-permute-start.1 = (bf16[128,16,128]{2,1,0:T(8,128)(2,1)S(1)}, bf16[128,16,128]{2,1,0:T(8,128)(2,1)S(1)}, u32[]{:S(2)}, u32[]{:S(2)}) collective-permute-start(bf16[128,16,128]{2,1,0:T(8,128)(2,1)S(1)} %all_to_all.22.own), channel_id=1, source_target_pairs={{0,16},{16,0},{32,48},{48,32},{64,80},{80,64},{96,112},{112,96},{1... | collective-permute-start | bytes 1572872 | tf_op jit(solution)/shard_map/ppermute | solution.py:32
  93.0 20.9 %copy-start.5 = (bf16[128,1024]{1,0:T(8,128)(2,1)S(1)}, bf16[128,1024]{1,0:T(8,128)(2,1)}, u32[]{:S(2)}) copy-start(bf16[128,1024]{1,0:T(8,128)(2,1)} %up.1) | copy-start | bytes 786436
  93.0 20.9 %copy-start.6 = (bf16[512,128]{1,0:T(8,128)(2,1)S(1)}, bf16[512,128]{1,0:T(8,128)(2,1)}, u32[]{:S(2)}) copy-start(bf16[512,128]{1,0:T(8,128)(2,1)} %down.1) | copy-start | bytes 393220

commit v3 on v0

v3 whole, which is shorter than its diff:
```python
import jax
import jax.numpy as jnp
from jax import lax
from jax.experimental import pallas as pl
from jax.experimental.pallas import tpu as pltpu
from jax.sharding import PartitionSpec as P

F32 = jnp.float32
BF16 = jnp.bfloat16
WIDTH = 128
SIDE = 32
STEPS = 8
FOLD = 4
PAIRS = 8
COLS = 16
HALF = PAIRS * SIDE
FULL = 2 * HALF

PARITY = [[(2 * a + core) * COLS + q for q in range(COLS) for a in range(PAIRS)] for core in (0, 1)]


def member(a, q):
    return q * PAIRS + a


def exchange(values):
    return lax.all_to_all(values, ("row", "col"), 0, 0, axis_index_groups=PARITY)


def swap_cores(values):
    return lax.ppermute(values, "row", [(i, i ^ 1) for i in range(2 * PAIRS)])


def core_index():
    return lax.rem(lax.axis_index("row"), 2)


def sigmoid(x):
    return 0.5 + 0.5 * jnp.tanh(0.5 * x)


def layer_norm(values, gain, bias):
    mean = jnp.mean(values, axis=0, keepdims=True)
    centred = values - mean
    var = jnp.mean(centred * centred, axis=0, keepdims=True)
    return centred * lax.rsqrt(var + 1e-05) * gain + bias


def dot(a, b):
    return lax.dot_general(a, b, (((1,), (0,)), ((), ())), preferred_element_type=F32)


def finish(field, mixed, gain, bias, weight, gate):
    mixnorm = layer_norm(mixed, gain, bias).astype(BF16)
    return field + gate * dot(weight, mixnorm)


def take_mixed(mixed, scratch):
    scratch[...] = mixed[...].astype(F32).reshape(WIDTH * STEPS, 128)
    steps = [scratch[pl.ds(step, WIDTH, stride=STEPS), :] for step in range(STEPS)]
    return jnp.concatenate(steps, axis=1)


def field_of(pair):
    rows = pair[...].astype(F32)
    steps = [rows[:, i].reshape(FOLD * SIDE, WIDTH).T for i in range(STEPS)]
    return jnp.concatenate(steps, axis=1)


def columns_of(refs):
    rows = jnp.concatenate([ref[...] for ref in refs], axis=0)
    rest = jnp.zeros((WIDTH - rows.shape[0], WIDTH), F32)
    return jnp.concatenate([rows, rest], axis=0).T


def factors_of(proj):
    h = WIDTH
    left = sigmoid(proj[:h]) * proj[h : 2 * h]
    right = sigmoid(proj[2 * h : 3 * h]) * proj[3 * h : 4 * h]
    return left, right


def put_factors(scratch, left, right, factors):
    for step in range(STEPS):
        lanes = slice(step * 128, (step + 1) * 128)
        scratch[pl.ds(step, WIDTH, stride=2 * STEPS), :] = left[:, lanes]
        scratch[pl.ds(step + STEPS, WIDTH, stride=2 * STEPS), :] = right[:, lanes]
    factors[...] = scratch[...].reshape(WIDTH, 2 * STEPS, 128).astype(BF16)


def first_kernel(
    pair_hbm, gain_hbm, bias_hbm, weight_hbm, factors, pair, gain, bias, weight, scratch, sems
):
    sources = (weight_hbm.at[0], pair_hbm, gain_hbm, bias_hbm)
    targets = (weight, pair, gain, bias)
    copies = [
        pltpu.make_async_copy(source, target, sems.at[i])
        for i, (source, target) in enumerate(zip(sources, targets))
    ]
    for copy in copies:
        copy.start()
    for copy in copies:
        copy.wait()
    vectors = columns_of((gain, bias))
    normed = layer_norm(field_of(pair), vectors[:, 0:1], vectors[:, 3:4]).astype(BF16)
    left, right = factors_of(dot(weight[:, : 4 * WIDTH].T, normed))
    put_factors(scratch, left, right, factors)


def gate_kernel(
    pair, norm_gain, norm_bias, out_gain, out_bias, weight, _, gates, fields, vectors
):
    vectors[...] = columns_of((norm_gain, norm_bias, out_gain, out_bias))
    field = field_of(pair)
    normed = layer_norm(field, vectors[:, 0:1], vectors[:, 3:4]).astype(BF16)
    gates[...] = sigmoid(dot(weight[0, :, 4 * WIDTH :].T, normed))
    fields[...] = field


def middle_kernel(
    mixed, gates, fields, vectors, weight, out_weight, factors, fields_out, scratch, product
):
    gain, bias = vectors[:, 1:2], vectors[:, 4:5]
    mix_gain, mix_bias = vectors[:, 6:7], vectors[:, 8:9]
    field = finish(
        fields[...], take_mixed(mixed, product), mix_gain, mix_bias, out_weight[0].T, gates[...]
    )
    normed = layer_norm(field, gain, bias).astype(BF16)
    put_factors(scratch, *factors_of(dot(weight[1, :, : 4 * WIDTH].T, normed)), factors)
    fields_out[...] = field


def second_gate_kernel(fields, vectors, weight, _, gates):
    normed = layer_norm(fields[...], vectors[:, 1:2], vectors[:, 4:5]).astype(BF16)
    gates[...] = sigmoid(dot(weight[1, :, 4 * WIDTH :].T, normed))


def last_kernel(mixed, gates, fields, vectors, out_weight, up, down, updated, product):
    gain, bias = vectors[:, 2:3], vectors[:, 5:6]
    mix_gain, mix_bias = vectors[:, 7:8], vectors[:, 9:10]
    inner = down.shape[0]
    field = finish(
        fields[...], take_mixed(mixed, product), mix_gain, mix_bias, out_weight[1].T, gates[...]
    )
    expanded = dot(up[...].T, layer_norm(field, gain, bias).astype(BF16))
    wide = expanded[:inner]
    act = (wide * sigmoid(wide) * expanded[inner:]).astype(BF16)
    field = field + dot(down[...].T, act)
    for i in range(STEPS):
        block = field[:, i * 128 : (i + 1) * 128].T.reshape(FOLD, SIDE, WIDTH)
        updated[:, i] = block.astype(BF16)


def turn(tiles):
    lane = lax.broadcasted_iota(jnp.int32, tiles[0].shape, 1)
    low = lane < 64
    even = (lane & 32) == 0

    def far(a, b):
        moved = pltpu.roll(jnp.where(low, b, a), 64, 1)
        return jnp.where(low, a, moved), jnp.where(low, moved, b)

    def near(a, b):
        return (
            jnp.where(even, a, pltpu.roll(b, 32, 1)),
            jnp.where(even, pltpu.roll(a, 96, 1), b),
        )

    a, b, c, d = tiles
    a, c = far(a, c)
    b, d = far(b, d)
    return *near(a, b), *near(c, d)


def lanes_from(g):
    return slice(g * 128, (g + 1) * 128)


def rows_of(source, columns, half):
    rows = slice(half * STEPS, (half + 1) * STEPS)
    tiles = [
        source[pl.ds(member(0, q), PAIRS), rows, :].astype(F32).reshape(PAIRS * STEPS, 128)
        for q in columns
    ]
    tiles = [tile.reshape(PAIRS, 1, STEPS, 128) for tile in turn(tiles)]
    return jnp.concatenate(tiles, axis=1)


def flat_rows(block):
    return block.reshape(HALF, 128).astype(BF16)


def send_product(mixed, product):
    mixed = mixed.reshape(PAIRS, FOLD, STEPS, FULL)
    for g in range(COLS // FOLD):
        tiles = [mixed[:, i, :, lanes_from(g)].reshape(PAIRS * STEPS, 128) for i in range(FOLD)]
        for i, tile in enumerate(turn(tiles)):
            rows = pl.ds(member(0, g * FOLD + i), PAIRS)
            product[rows] = tile.reshape(PAIRS, STEPS, 128).astype(BF16)


def outgoing_kernel(own, other, _, product, left, right):
    core = core_index()
    for g in range(COLS // FOLD):
        columns = [g * FOLD + i for i in range(FOLD)]
        left[:, lanes_from(g)] = flat_rows(rows_of(own, columns, 0))
        for source, parity in ((own, core), (other, 1 - core)):
            block = rows_of(source, columns, 1).reshape(PAIRS, SIDE, 128).astype(BF16)
            right[:, parity, :, lanes_from(g)] = block
    mixed = lax.dot_general(
        left[...], right[...].reshape(FULL, FULL), (((1,), (1,)), ((), ())),
        preferred_element_type=F32,
    )
    send_product(mixed, product)


def incoming_kernel(own, other, _, product, left, right):
    core = core_index()
    for part, source in enumerate((own, other)):
        rows = slice(part * HALF, (part + 1) * HALF)
        for g in range(COLS // FOLD):
            columns = [g * FOLD + i for i in range(FOLD)]
            right[rows, lanes_from(g)] = flat_rows(rows_of(source, columns, 1))
        for g in range(PAIRS // FOLD):
            columns = [2 * (g * FOLD + i) + core for i in range(FOLD)]
            left[rows, lanes_from(g)] = flat_rows(rows_of(source, columns, 0))
    mixed = lax.dot_general(
        left[...], right[...], (((0,), (0,)), ((), ())), preferred_element_type=F32
    )
    send_product(mixed, product)


def call(kernel, outs, scratch, name, vmem=40, **more):
    return pl.pallas_call(
        kernel,
        out_shape=outs,
        scratch_shapes=scratch,
        compiler_params=pltpu.CompilerParams(vmem_limit_bytes=vmem * 1024 * 1024),
        name=name,
        **more,
    )


def shape(*dims, dtype=BF16):
    return jax.ShapeDtypeStruct(dims, dtype)


def body(
    pair, norm_gain, norm_bias, proj_weight, out_gain, out_bias, out_weight, up_weight, down_weight
):
    flat = shape(WIDTH, STEPS * 128, dtype=F32)
    packed = shape(WIDTH, 2 * STEPS, 128)
    product = shape(WIDTH, STEPS, 128)
    packing = pltpu.VMEM((WIDTH * 2 * STEPS, 128), F32)
    unpacking = pltpu.VMEM((WIDTH * STEPS, 128), F32)
    blocks = (FOLD, STEPS, SIDE, WIDTH)

    pair = pair.reshape(blocks)
    operands = (pair, norm_gain, norm_bias)
    landing = [pltpu.VMEM(v.shape, v.dtype) for v in operands]
    landing += [pltpu.VMEM(proj_weight.shape[1:], BF16), packing, pltpu.SemaphoreType.DMA((4,))]
    hbm = pl.BlockSpec(memory_space=pltpu.HBM)
    vmem = pl.BlockSpec(memory_space=pltpu.VMEM)
    after = pl.BlockSpec(memory_space=pl.ANY)
    factors = call(first_kernel, packed, landing, "first", 60, in_specs=[hbm] * 4)(
        *operands, proj_weight
    )
    own = exchange(factors)
    other = swap_cores(own)
    gate, field, vectors = call(
        gate_kernel, (flat, flat, shape(WIDTH, WIDTH, dtype=F32)), [], "gate",
        in_specs=[vmem] * 6 + [after],
    )(pair, norm_gain, norm_bias, out_gain, out_bias, proj_weight, own)
    left, right = pltpu.VMEM((HALF, FULL), BF16), pltpu.VMEM((PAIRS, 2, SIDE, FULL), BF16)
    mixed = call(
        outgoing_kernel, product, [left, right], "outgoing", in_specs=[vmem, vmem, after]
    )(own, other, vectors)
    factors, field = call(middle_kernel, (packed, flat), [packing, unpacking], "middle")(
        exchange(mixed), gate, field, vectors, proj_weight, out_weight
    )
    own = exchange(factors)
    other = swap_cores(own)
    gate = call(second_gate_kernel, flat, [], "second_gate", in_specs=[vmem] * 3 + [after])(
        field, vectors, proj_weight, own
    )
    left, right = pltpu.VMEM((FULL, HALF), BF16), pltpu.VMEM((FULL, FULL), BF16)
    mixed = call(
        incoming_kernel, product, [left, right], "incoming", in_specs=[vmem, vmem, after]
    )(own, other, gate)
    updated = call(last_kernel, shape(*blocks), [unpacking], "last")(
        exchange(mixed), gate, field, vectors, out_weight, up_weight, down_weight
    )
    return updated.reshape(FOLD * STEPS, SIDE, WIDTH)


def solution(mesh):
    placed = (P("row", "col", None), P(), P(), P(), P(), P(), P(), P(), P())
    return jax.shard_map(
        body, mesh=mesh, in_specs=placed, out_specs=P("row", "col", None), check_vma=False
    )
```

time: 747 us -> 115 us (0.15)
  waiting for transfers between devices: 658 us -> 2.93 us
  blocking collectives: 0 us -> 102 us
  local copies, waits for them, and re-layouts: 41.5 us -> 0.06 us
  matrix products: 19 us -> 0 us
  between operations: 13.7 us -> 0.16 us
  other arithmetic: 12.9 us -> 0 us
  Pallas kernels: 0 us -> 9.77 us
    psum x2 -> x0, waiting for transfers between devices: 349 us -> none  [spread(): return lax.psum(kept, axis)]
    all_gather x4 -> x0, waiting for transfers between devices: 308 us -> none  [the longest x1 101 us: body(): lax.all_gather(right, 'col', axis=1, tiled=True)]
    all_to_all x0 -> x4, blocking collectives: none -> 102 us  [exchange(): lax.all_to_all(values, ('row', 'col'), 0, 0, axis_index_groups=PARITY)]
    all_gather x3 -> x0, local copies, waits for them, and re-layouts: 25.1 us -> none  [the longest x1 8.6 us: body(): lax.all_gather(left, 'row', axis=0, tiled=True)]
    dot_general x8 -> x0, matrix products: 19 us -> none  [the longest x1 6.13 us: body(): jnp.einsum('ikc,jkc->ijc', left_rows, pieces, preferred_element_type=jnp....]
    pallas_call x0 -> x7, Pallas kernels: none -> 9.77 us  [the longest x1 2.8 us: body(): call(first_kernel, packed, landing, 'first', 60, in_specs=[hbm] * 4)]
    psum x1 -> x0, local copies, waits for them, and re-layouts: 7.99 us -> none  [spread(): return lax.psum(kept, axis)]
  transfers between devices with their start and end apart: 6 -> 2, of which waited for: 6 -> 2; matrix products, arithmetic and copies ran while one was open for 4% -> 0% of each run, Pallas kernels for 0% -> 1%
where the time goes in v3:
time: 115 us
  blocking collectives  102 us (89%)
  Pallas kernels  9.77 us (8%)
  waiting for transfers between devices  2.93 us (3%)
    all_to_all x4, blocking collectives, exchange(): lax.all_to_all(values, ('row', 'col'), 0, 0, axis_index_groups=PARITY)  102 us
    ppermute x2, waiting for transfers between devices, swap_cores(): return lax.ppermute(values, 'row', [(i, i ^ 1) for i in range(2 * PAIRS)])  2.93 us
    pallas_call x1, Pallas kernels, body(): call(first_kernel, packed, landing, 'first', 60, in_specs=[hbm] * 4)  2.8 us
  transfers between devices with their start and end apart: 2, of which 2 were waited for; matrix products, arithmetic and copies ran while one was open for 0% of the time, Pallas kernels for 1%

profile of v3, /device:TPU:2, one launch (start us, length us, event | category | flops | bytes accessed | tf_op | source)
XLA Modules:
  0.0 114.9 jit_solution(1831189343923739890)
XLA Ops:
  0.0 2.8 %first.1 = bf16[128,16,128]{2,1,0:T(8,128)(2,1)} custom-call(bf16[4,8,32,128]{3,2,1,0:T(8,128)(2,1)} %bitcast.2, f32[3,128]{1,0:T(4,128)} %norm_gain.1, f32[3,128]{1,0:T(4,128)} %norm_bias.1, bf16[2,128,640]{2,1,0:T(8,128)(2,1)} %weight.5), custom_call_target="tpu_custom_call" | custom-call | tf_op jit(solution)/shard_map/first/pallas_call | solution.py:265
  2.8 0.0 copy-start
  2.8 0.0 copy-start.1
  2.8 0.0 copy-start.5
  2.8 0.0 copy-start.6
  2.9 0.0 copy-start.7
  2.9 0.0 copy-start.8
  2.9 35.1 %all_to_all.20._.own = bf16[128,16,128]{2,1,0:T(8,128)(2,1)S(1)} all-to-all(bf16[128,16,128]{2,1,0:T(8,128)(2,1)} %first.1), channel_id=1, replica_groups={{0,32,64,96,128,160,192,224,1,33,65,97,129,161,193,225,2,34,66,98,130,1..., dimensions={0} | all-to-all | bytes 1048576 | tf_op jit(solution)/shard_map/all_to_all | solution.py:27
  38.0 0.0 collective-permute-start
  38.0 0.0 copy-done
  38.0 0.0 copy-done.1
  38.0 0.0 copy-done.5
  38.0 0.0 copy-done.6
  38.0 0.0 copy-done.7
  38.0 0.0 copy-done.8
  38.0 0.5 gate.1
  38.5 1.4 %collective-permute-done.other = bf16[128,16,128]{2,1,0:T(8,128)(2,1)S(1)} collective-permute-done((bf16[128,16,128]{2,1,0:T(8,128)(2,1)S(1)}, bf16[128,16,128]{2,1,0:T(8,128)(2,1)S(1)}, u32[]{:S(2)}, u32[]{:S(2)}) %collective-permute-start) | collective-permute-done | bytes 524320 | tf_op jit(solution)/shard_map/ppermute | solution.py:31
  39.9 1.3 %outgoing.1 = bf16[128,8,128]{2,1,0:T(8,128)(2,1)S(1)} custom-call(bf16[128,16,128]{2,1,0:T(8,128)(2,1)S(1)} %all_to_all.20._.own, bf16[128,16,128]{2,1,0:T(8,128)(2,1)S(1)} %collective-permute-done.other, f32[128,128]{1,0:T(8,128)S(1)} %get-tuple-element.10._.vectors), custom_call_target="tpu_custom_call" | custom-call | tf_op jit(solution)/shard_map/outgoing/pallas_call | solution.py:275
  41.2 0.0 copy-start.2
  41.2 20.9 %all_to_all.21.mixed = bf16[128,8,128]{2,1,0:T(8,128)(2,1)S(1)} all-to-all(bf16[128,8,128]{2,1,0:T(8,128)(2,1)S(1)} %outgoing.1), channel_id=1, replica_groups={{0,32,64,96,128,160,192,224,1,33,65,97,129,161,193,225,2,34,66,98,130,1..., dimensions={0} | all-to-all | bytes 524288 | tf_op jit(solution)/shard_map/all_to_all | solution.py:27
  62.1 0.0 copy-done.2
  62.1 1.1 middle.1
  63.2 25.1 %all_to_all.22._.own = bf16[128,16,128]{2,1,0:T(8,128)(2,1)S(1)} all-to-all(bf16[128,16,128]{2,1,0:T(8,128)(2,1)S(1)} %get-tuple-element.13), channel_id=1, replica_groups={{0,32,64,96,128,160,192,224,1,33,65,97,129,161,193,225,2,34,66,98,130,1..., dimensions={0} | all-to-all | bytes 1048576 | tf_op jit(solution)/shard_map/all_to_all | solution.py:27
  88.3 0.0 collective-permute-start.1
  88.3 0.4 second_gate.1._.gates
  88.6 1.5 %collective-permute-done.1.other = bf16[128,16,128]{2,1,0:T(8,128)(2,1)S(1)} collective-permute-done((bf16[128,16,128]{2,1,0:T(8,128)(2,1)S(1)}, bf16[128,16,128]{2,1,0:T(8,128)(2,1)S(1)}, u32[]{:S(2)}, u32[]{:S(2)}) %collective-permute-start.1) | collective-permute-done | bytes 524320 | tf_op jit(solution)/shard_map/ppermute | solution.py:31
  90.2 1.5 %incoming.1 = bf16[128,8,128]{2,1,0:T(8,128)(2,1)S(1)} custom-call(bf16[128,16,128]{2,1,0:T(8,128)(2,1)S(1)} %all_to_all.22._.own, bf16[128,16,128]{2,1,0:T(8,128)(2,1)S(1)} %collective-permute-done.1.other, f32[128,1024]{1,0:T(8,128)S(1)} %second_gate.1._.gates), custom_call_target="tpu_custom_call" | custom-call | tf_op jit(solution)/shard_map/incoming/pallas_call | solution.py:287
  91.7 0.0 copy-start.3
  91.7 0.0 copy-start.4
  91.8 21.0 %all_to_all.23.mixed = bf16[128,8,128]{2,1,0:T(8,128)(2,1)S(1)} all-to-all(bf16[128,8,128]{2,1,0:T(8,128)(2,1)S(1)} %incoming.1), channel_id=1, replica_groups={{0,32,64,96,128,160,192,224,1,33,65,97,129,161,193,225,2,34,66,98,130,1..., dimensions={0} | all-to-all | bytes 524288 | tf_op jit(solution)/shard_map/all_to_all | solution.py:27
  112.8 0.0 copy-done.3
  112.8 2.1 %last.1 = bf16[4,8,32,128]{3,2,1,0:T(8,128)(2,1)} custom-call(bf16[128,8,128]{2,1,0:T(8,128)(2,1)S(1)} %all_to_all.23.mixed, f32[128,1024]{1,0:T(8,128)S(1)} %second_gate.1._.gates, f32[128,1024]{1,0:T(8,128)S(1)} %get-tuple-element.14.fields, f32[128,128]{1,0:T(8,128)S(1)} %get-tuple-element.10._.vectors, bf16[2,128,128]{2,1,0:T(8,128)(2,1)S(1)} %copy-done.2, ...), custom_call_target="tpu_custom_call" | custom-call | tf_op jit(solution)/shard_map/last/pallas_call | solution.py:290
  (1 shorter events, 0.0 us)
Async XLA Ops:
  2.8 35.2 %copy-start = (bf16[2,128,640]{2,1,0:T(8,128)(2,1)S(1)}, bf16[2,128,640]{2,1,0:T(8,128)(2,1)}, u32[]{:S(2)}) copy-start(bf16[2,128,640]{2,1,0:T(8,128)(2,1)} %weight.5) | copy-start | bytes 983044
  2.8 35.1 %copy-start.1 = (bf16[32,32,128]{2,1,0:T(8,128)(2,1)S(1)}, bf16[32,32,128]{2,1,0:T(8,128)(2,1)}, u32[]{:S(2)}) copy-start(bf16[32,32,128]{2,1,0:T(8,128)(2,1)} %param.9) | copy-start | bytes 786436
  2.8 35.1 %copy-start.5 = (f32[3,128]{1,0:T(4,128)S(1)}, f32[3,128]{1,0:T(4,128)}, u32[]{:S(2)}) copy-start(f32[3,128]{1,0:T(4,128)} %norm_gain.1) | copy-start | bytes 4612
  2.8 35.1 %copy-start.6 = (f32[3,128]{1,0:T(4,128)S(1)}, f32[3,128]{1,0:T(4,128)}, u32[]{:S(2)}) copy-start(f32[3,128]{1,0:T(4,128)} %norm_bias.1) | copy-start | bytes 4612
  2.9 35.1 %copy-start.7 = (f32[2,128]{1,0:T(2,128)S(1)}, f32[2,128]{1,0:T(2,128)}, u32[]{:S(2)}) copy-start(f32[2,128]{1,0:T(2,128)} %out_gain.1) | copy-start | bytes 3076
  2.9 35.1 %copy-start.8 = (f32[2,128]{1,0:T(2,128)S(1)}, f32[2,128]{1,0:T(2,128)}, u32[]{:S(2)}) copy-start(f32[2,128]{1,0:T(2,128)} %out_bias.1) | copy-start | bytes 3076
  38.0 1.9 %collective-permute-start = (bf16[128,16,128]{2,1,0:T(8,128)(2,1)S(1)}, bf16[128,16,128]{2,1,0:T(8,128)(2,1)S(1)}, u32[]{:S(2)}, u32[]{:S(2)}) collective-permute-start(bf16[128,16,128]{2,1,0:T(8,128)(2,1)S(1)} %all_to_all.20._.own), channel_id=1, source_target_pairs={{0,16},{16,0},{32,48},{48,32},{64,80},{80,64},{96,112},{112,96},{1... | collective-permute-start | bytes 1572872 | tf_op jit(solution)/shard_map/ppermute | solution.py:31
  41.2 20.9 %copy-start.2 = (bf16[2,128,128]{2,1,0:T(8,128)(2,1)S(1)}, bf16[2,128,128]{2,1,0:T(8,128)(2,1)}, u32[]{:S(2)}) copy-start(bf16[2,128,128]{2,1,0:T(8,128)(2,1)} %out_weight.3) | copy-start | bytes 196612
  88.3 1.9 %collective-permute-start.1 = (bf16[128,16,128]{2,1,0:T(8,128)(2,1)S(1)}, bf16[128,16,128]{2,1,0:T(8,128)(2,1)S(1)}, u32[]{:S(2)}, u32[]{:S(2)}) collective-permute-start(bf16[128,16,128]{2,1,0:T(8,128)(2,1)S(1)} %all_to_all.22._.own), channel_id=1, source_target_pairs={{0,16},{16,0},{32,48},{48,32},{64,80},{80,64},{96,112},{112,96},{1... | collective-permute-start | bytes 1572872 | tf_op jit(solution)/shard_map/ppermute | solution.py:31
  91.7 21.1 %copy-start.3 = (bf16[128,1024]{1,0:T(8,128)(2,1)S(1)}, bf16[128,1024]{1,0:T(8,128)(2,1)}, u32[]{:S(2)}) copy-start(bf16[128,1024]{1,0:T(8,128)(2,1)} %up.1) | copy-start | bytes 786436
  91.7 21.0 %copy-start.4 = (bf16[512,128]{1,0:T(8,128)(2,1)S(1)}, bf16[512,128]{1,0:T(8,128)(2,1)}, u32[]{:S(2)}) copy-start(bf16[512,128]{1,0:T(8,128)(2,1)} %down.1) | copy-start | bytes 393220

commit v4 on v3

--- a/solution.py
+++ b/solution.py
@@ -107,16 +107,6 @@
     put_factors(scratch, left, right, factors)
 
 
-def gate_kernel(
-    pair, norm_gain, norm_bias, out_gain, out_bias, weight, _, gates, fields, vectors
-):
-    vectors[...] = columns_of((norm_gain, norm_bias, out_gain, out_bias))
-    field = field_of(pair)
-    normed = layer_norm(field, vectors[:, 0:1], vectors[:, 3:4]).astype(BF16)
-    gates[...] = sigmoid(dot(weight[0, :, 4 * WIDTH :].T, normed))
-    fields[...] = field
-
-
 def middle_kernel(
     mixed, gates, fields, vectors, weight, out_weight, factors, fields_out, scratch, product
 ):
@@ -128,11 +118,6 @@
     normed = layer_norm(field, gain, bias).astype(BF16)
     put_factors(scratch, *factors_of(dot(weight[1, :, : 4 * WIDTH].T, normed)), factors)
     fields_out[...] = field
-
-
-def second_gate_kernel(fields, vectors, weight, _, gates):
-    normed = layer_norm(fields[...], vectors[:, 1:2], vectors[:, 4:5]).astype(BF16)
-    gates[...] = sigmoid(dot(weight[1, :, 4 * WIDTH :].T, normed))
 
 
 def last_kernel(mixed, gates, fields, vectors, out_weight, up, down, updated, product):
@@ -190,44 +175,65 @@
     return block.reshape(HALF, 128).astype(BF16)
 
 
-def send_product(mixed, product):
-    mixed = mixed.reshape(PAIRS, FOLD, STEPS, FULL)
-    for g in range(COLS // FOLD):
+def send_product(mixed, product, columns):
+    mixed = mixed.reshape(PAIRS, FOLD, STEPS, SIDE * len(columns))
+    for g in range(len(columns) // FOLD):
         tiles = [mixed[:, i, :, lanes_from(g)].reshape(PAIRS * STEPS, 128) for i in range(FOLD)]
         for i, tile in enumerate(turn(tiles)):
-            rows = pl.ds(member(0, g * FOLD + i), PAIRS)
+            rows = pl.ds(member(0, columns[g * FOLD + i]), PAIRS)
             product[rows] = tile.reshape(PAIRS, STEPS, 128).astype(BF16)
 
 
-def outgoing_kernel(own, other, _, product, left, right):
+def outgoing_own_kernel(
+    own, pair, norm_gain, norm_bias, out_gain, out_bias, weight,
+    left, right, gates, fields, vectors,
+):
+    for g in range(COLS // FOLD):
+        columns = [g * FOLD + i for i in range(FOLD)]
+        left[:, lanes_from(g)] = flat_rows(rows_of(own, columns, 0))
+        right[:, lanes_from(g)] = flat_rows(rows_of(own, columns, 1))
+    vectors[...] = columns_of((norm_gain, norm_bias, out_gain, out_bias))
+    field = field_of(pair)
+    normed = layer_norm(field, vectors[:, 0:1], vectors[:, 3:4]).astype(BF16)
+    gates[...] = sigmoid(dot(weight[0, :, 4 * WIDTH :].T, normed))
+    fields[...] = field
+
+
+def outgoing_kernel(other, left, right_own, product, right):
     core = core_index()
     for g in range(COLS // FOLD):
         columns = [g * FOLD + i for i in range(FOLD)]
-        left[:, lanes_from(g)] = flat_rows(rows_of(own, columns, 0))
-        for source, parity in ((own, core), (other, 1 - core)):
-            block = rows_of(source, columns, 1).reshape(PAIRS, SIDE, 128).astype(BF16)
-            right[:, parity, :, lanes_from(g)] = block
-    mixed = lax.dot_general(
-        left[...], right[...].reshape(FULL, FULL), (((1,), (1,)), ((), ())),
-        preferred_element_type=F32,
-    )
-    send_product(mixed, product)
-
-
-def incoming_kernel(own, other, _, product, left, right):
+        right[:, lanes_from(g)] = flat_rows(rows_of(other, columns, 1))
+    for factor, parity in ((right_own, core), (right, 1 - core)):
+        mixed = lax.dot_general(
+            left[...], factor[...], (((1,), (1,)), ((), ())), preferred_element_type=F32
+        )
+        send_product(mixed, product, [2 * a + parity for a in range(PAIRS)])
+
+
+def form_incoming(source, left, right):
     core = core_index()
-    for part, source in enumerate((own, other)):
-        rows = slice(part * HALF, (part + 1) * HALF)
-        for g in range(COLS // FOLD):
-            columns = [g * FOLD + i for i in range(FOLD)]
-            right[rows, lanes_from(g)] = flat_rows(rows_of(source, columns, 1))
-        for g in range(PAIRS // FOLD):
-            columns = [2 * (g * FOLD + i) + core for i in range(FOLD)]
-            left[rows, lanes_from(g)] = flat_rows(rows_of(source, columns, 0))
-    mixed = lax.dot_general(
-        left[...], right[...], (((0,), (0,)), ((), ())), preferred_element_type=F32
-    )
-    send_product(mixed, product)
+    for g in range(COLS // FOLD):
+        columns = [g * FOLD + i for i in range(FOLD)]
+        right[:, lanes_from(g)] = flat_rows(rows_of(source, columns, 1))
+    for g in range(PAIRS // FOLD):
+        columns = [2 * (g * FOLD + i) + core for i in range(FOLD)]
+        left[:, lanes_from(g)] = flat_rows(rows_of(source, columns, 0))
+
+
+def incoming_own_kernel(own, fields, vectors, weight, left, right, gates):
+    form_incoming(own, left, right)
+    normed = layer_norm(fields[...], vectors[:, 1:2], vectors[:, 4:5]).astype(BF16)
+    gates[...] = sigmoid(dot(weight[1, :, 4 * WIDTH :].T, normed))
+
+
+def incoming_kernel(other, left_own, right_own, product, left, right):
+    form_incoming(other, left, right)
+    mixed = sum(
+        lax.dot_general(a[...], b[...], (((0,), (0,)), ((), ())), preferred_element_type=F32)
+        for a, b in ((left_own, right_own), (left, right))
+    )
+    send_product(mixed, product, range(COLS))
 
 
 def call(kernel, outs, scratch, name, vmem=40, **more):
@@ -235,7 +241,7 @@
         kernel,
         out_shape=outs,
         scratch_shapes=scratch,
-        compiler_params=pltpu.CompilerParams(vmem_limit_bytes=vmem * 1024 * 1024),
+        compiler_params=pltpu.CompilerParams(vmem_limit_bytes=int(vmem * 1024 * 1024)),
         name=name,
         **more,
     )
@@ -260,33 +266,30 @@
     landing = [pltpu.VMEM(v.shape, v.dtype) for v in operands]
     landing += [pltpu.VMEM(proj_weight.shape[1:], BF16), packing, pltpu.SemaphoreType.DMA((4,))]
     hbm = pl.BlockSpec(memory_space=pltpu.HBM)
-    vmem = pl.BlockSpec(memory_space=pltpu.VMEM)
-    after = pl.BlockSpec(memory_space=pl.ANY)
     factors = call(first_kernel, packed, landing, "first", 60, in_specs=[hbm] * 4)(
         *operands, proj_weight
     )
     own = exchange(factors)
     other = swap_cores(own)
-    gate, field, vectors = call(
-        gate_kernel, (flat, flat, shape(WIDTH, WIDTH, dtype=F32)), [], "gate",
-        in_specs=[vmem] * 6 + [after],
-    )(pair, norm_gain, norm_bias, out_gain, out_bias, proj_weight, own)
-    left, right = pltpu.VMEM((HALF, FULL), BF16), pltpu.VMEM((PAIRS, 2, SIDE, FULL), BF16)
-    mixed = call(
-        outgoing_kernel, product, [left, right], "outgoing", in_specs=[vmem, vmem, after]
-    )(own, other, vectors)
+    wide, square = (HALF, FULL), (HALF, HALF)
+    outs = (shape(*wide), shape(*wide), flat, flat, shape(WIDTH, WIDTH, dtype=F32))
+    left, right, gate, field, vectors = call(outgoing_own_kernel, outs, [], "outgoing_own")(
+        own, pair, norm_gain, norm_bias, out_gain, out_bias, proj_weight
+    )
+    mixed = call(outgoing_kernel, product, [pltpu.VMEM(wide, BF16)], "outgoing")(
+        other, left, right
+    )
     factors, field = call(middle_kernel, (packed, flat), [packing, unpacking], "middle")(
         exchange(mixed), gate, field, vectors, proj_weight, out_weight
     )
     own = exchange(factors)
     other = swap_cores(own)
-    gate = call(second_gate_kernel, flat, [], "second_gate", in_specs=[vmem] * 3 + [after])(
-        field, vectors, proj_weight, own
-    )
-    left, right = pltpu.VMEM((FULL, HALF), BF16), pltpu.VMEM((FULL, FULL), BF16)
-    mixed = call(
-        incoming_kernel, product, [left, right], "incoming", in_specs=[vmem, vmem, after]
-    )(own, other, gate)
+    outs = (shape(*square), shape(*wide), flat)
+    left, right, gate = call(incoming_own_kernel, outs, [], "incoming_own")(
+        own, field, vectors, proj_weight
+    )
+    forming = [pltpu.VMEM(square, BF16), pltpu.VMEM(wide, BF16)]
+    mixed = call(incoming_kernel, product, forming, "incoming")(other, left, right)
     updated = call(last_kernel, shape(*blocks), [unpacking], "last")(
         exchange(mixed), gate, field, vectors, out_weight, up_weight, down_weight
     )

time: 115 us -> 114 us (level)
  transfers between devices with their start and end apart: 2 -> 2, of which waited for: 2 -> 2; matrix products, arithmetic and copies ran while one was open for 0% -> 0% of each run, Pallas kernels for 1% -> 2%
where the time goes in v4:
time: 114 us
  blocking collectives  102 us (89%)
  Pallas kernels  9.42 us (8%)
  waiting for transfers between devices  1.95 us (2%)
    all_to_all x4, blocking collectives, exchange(): lax.all_to_all(values, ('row', 'col'), 0, 0, axis_index_groups=PARITY)  102 us
    pallas_call x1, Pallas kernels, body(): call(first_kernel, packed, landing, 'first', 60, in_specs=[hbm] * 4)  2.79 us
  transfers between devices with their start and end apart: 2, of which 2 were waited for; matrix products, arithmetic and copies ran while one was open for 0% of the time, Pallas kernels for 2%

profile of v4, /device:TPU:2, one launch (start us, length us, event | category | flops | bytes accessed | tf_op | source)
XLA Modules:
  0.0 113.6 jit_solution(16726185953081318658)
XLA Ops:
  0.0 2.8 %first.1 = bf16[128,16,128]{2,1,0:T(8,128)(2,1)} custom-call(bf16[4,8,32,128]{3,2,1,0:T(8,128)(2,1)} %bitcast.2, f32[3,128]{1,0:T(4,128)} %norm_gain.1, f32[3,128]{1,0:T(4,128)} %norm_bias.1, bf16[2,128,640]{2,1,0:T(8,128)(2,1)} %weight.5), custom_call_target="tpu_custom_call" | custom-call | tf_op jit(solution)/shard_map/first/pallas_call | solution.py:269
  2.8 0.0 copy-start
  2.8 0.0 copy-start.1
  2.8 0.0 copy-start.5
  2.8 0.0 copy-start.6
  2.8 0.0 copy-start.7
  2.9 0.0 copy-start.8
  2.9 35.1 %all_to_all.20.own = bf16[128,16,128]{2,1,0:T(8,128)(2,1)S(1)} all-to-all(bf16[128,16,128]{2,1,0:T(8,128)(2,1)} %first.1), channel_id=1, replica_groups={{0,32,64,96,128,160,192,224,1,33,65,97,129,161,193,225,2,34,66,98,130,1..., dimensions={0} | all-to-all | bytes 1048576 | tf_op jit(solution)/shard_map/all_to_all | solution.py:27
  37.9 0.0 collective-permute-start
  38.0 0.0 copy-done
  38.0 0.0 copy-done.1
  38.0 0.0 copy-done.5
  38.0 0.0 copy-done.6
  38.0 0.0 copy-done.7
  38.0 0.0 copy-done.8
  38.0 1.2 %outgoing_own.1 = (bf16[256,512]{1,0:T(8,128)(2,1)S(1)}, bf16[256,512]{1,0:T(8,128)(2,1)S(1)}, f32[128,1024]{1,0:T(8,128)S(1)}, f32[128,1024]{1,0:T(8,128)S(1)}, f32[128,128]{1,0:T(8,128)S(1)}) custom-call(bf16[128,16,128]{2,1,0:T(8,128)(2,1)S(1)} %all_to_all.20.own, bf16[4,8,32,128]{3,2,1,0:T(8,128)(2,1)S(1)} %bitcast.3, f32[3,128]{1,0:T(4,128)S(1)} %copy-done.5, ...), custom_call_target="tpu_custom_call" | custom-call | tf_op jit(solution)/shard_map/outgoing_own/pallas_call | solution.py:276
  39.2 0.7 collective-permute-done.other
  39.9 0.7 outgoing.1
  40.6 0.0 copy-start.2
  40.6 20.8 %all_to_all.21.mixed = bf16[128,8,128]{2,1,0:T(8,128)(2,1)S(1)} all-to-all(bf16[128,8,128]{2,1,0:T(8,128)(2,1)S(1)} %outgoing.1), channel_id=1, replica_groups={{0,32,64,96,128,160,192,224,1,33,65,97,129,161,193,225,2,34,66,98,130,1..., dimensions={0} | all-to-all | bytes 524288 | tf_op jit(solution)/shard_map/all_to_all | solution.py:27
  61.5 0.0 copy-done.2
  61.5 1.1 middle.1
  62.6 25.1 %all_to_all.22.own = bf16[128,16,128]{2,1,0:T(8,128)(2,1)S(1)} all-to-all(bf16[128,16,128]{2,1,0:T(8,128)(2,1)S(1)} %get-tuple-element.20), channel_id=1, replica_groups={{0,32,64,96,128,160,192,224,1,33,65,97,129,161,193,225,2,34,66,98,130,1..., dimensions={0} | all-to-all | bytes 1048576 | tf_op jit(solution)/shard_map/all_to_all | solution.py:27
  87.7 0.0 collective-permute-start.1
  87.7 0.6 incoming_own.1
  88.3 1.3 %collective-permute-done.1.other = bf16[128,16,128]{2,1,0:T(8,128)(2,1)S(1)} collective-permute-done((bf16[128,16,128]{2,1,0:T(8,128)(2,1)S(1)}, bf16[128,16,128]{2,1,0:T(8,128)(2,1)S(1)}, u32[]{:S(2)}, u32[]{:S(2)}) %collective-permute-start.1) | collective-permute-done | bytes 524320 | tf_op jit(solution)/shard_map/ppermute | solution.py:31
  89.6 0.8 incoming.1
  90.4 0.0 copy-start.3
  90.4 0.0 copy-start.4
  90.4 21.0 %all_to_all.23.mixed = bf16[128,8,128]{2,1,0:T(8,128)(2,1)S(1)} all-to-all(bf16[128,8,128]{2,1,0:T(8,128)(2,1)S(1)} %incoming.1), channel_id=1, replica_groups={{0,32,64,96,128,160,192,224,1,33,65,97,129,161,193,225,2,34,66,98,130,1..., dimensions={0} | all-to-all | bytes 524288 | tf_op jit(solution)/shard_map/all_to_all | solution.py:27
  111.5 0.0 copy-done.3
  111.5 2.1 %last.1 = bf16[4,8,32,128]{3,2,1,0:T(8,128)(2,1)} custom-call(bf16[128,8,128]{2,1,0:T(8,128)(2,1)S(1)} %all_to_all.23.mixed, f32[128,1024]{1,0:T(8,128)S(1)} %get-tuple-element.24.gates, f32[128,1024]{1,0:T(8,128)S(1)} %get-tuple-element.21.fields, f32[128,128]{1,0:T(8,128)S(1)} %get-tuple-element.19.vectors, bf16[2,128,128]{2,1,0:T(8,128)(2,1)S(1)} %copy-done.2, ...), custom_call_target="tpu_custom_call" | custom-call | tf_op jit(solution)/shard_map/last/pallas_call | solution.py:293
  (1 shorter events, 0.0 us)
Async XLA Ops:
  2.8 35.2 %copy-start = (bf16[2,128,640]{2,1,0:T(8,128)(2,1)S(1)}, bf16[2,128,640]{2,1,0:T(8,128)(2,1)}, u32[]{:S(2)}) copy-start(bf16[2,128,640]{2,1,0:T(8,128)(2,1)} %weight.5) | copy-start | bytes 983044
  2.8 35.1 %copy-start.1 = (bf16[32,32,128]{2,1,0:T(8,128)(2,1)S(1)}, bf16[32,32,128]{2,1,0:T(8,128)(2,1)}, u32[]{:S(2)}) copy-start(bf16[32,32,128]{2,1,0:T(8,128)(2,1)} %param.9) | copy-start | bytes 786436
  2.8 35.1 %copy-start.5 = (f32[3,128]{1,0:T(4,128)S(1)}, f32[3,128]{1,0:T(4,128)}, u32[]{:S(2)}) copy-start(f32[3,128]{1,0:T(4,128)} %norm_gain.1) | copy-start | bytes 4612
  2.8 35.1 %copy-start.6 = (f32[3,128]{1,0:T(4,128)S(1)}, f32[3,128]{1,0:T(4,128)}, u32[]{:S(2)}) copy-start(f32[3,128]{1,0:T(4,128)} %norm_bias.1) | copy-start | bytes 4612
  2.8 35.1 %copy-start.7 = (f32[2,128]{1,0:T(2,128)S(1)}, f32[2,128]{1,0:T(2,128)}, u32[]{:S(2)}) copy-start(f32[2,128]{1,0:T(2,128)} %out_gain.1) | copy-start | bytes 3076
  2.9 35.1 %copy-start.8 = (f32[2,128]{1,0:T(2,128)S(1)}, f32[2,128]{1,0:T(2,128)}, u32[]{:S(2)}) copy-start(f32[2,128]{1,0:T(2,128)} %out_bias.1) | copy-start | bytes 3076
  37.9 1.9 %collective-permute-start = (bf16[128,16,128]{2,1,0:T(8,128)(2,1)S(1)}, bf16[128,16,128]{2,1,0:T(8,128)(2,1)S(1)}, u32[]{:S(2)}, u32[]{:S(2)}) collective-permute-start(bf16[128,16,128]{2,1,0:T(8,128)(2,1)S(1)} %all_to_all.20.own), channel_id=1, source_target_pairs={{0,16},{16,0},{32,48},{48,32},{64,80},{80,64},{96,112},{112,96},{1... | collective-permute-start | bytes 1572872 | tf_op jit(solution)/shard_map/ppermute | solution.py:31
  40.6 20.9 %copy-start.2 = (bf16[2,128,128]{2,1,0:T(8,128)(2,1)S(1)}, bf16[2,128,128]{2,1,0:T(8,128)(2,1)}, u32[]{:S(2)}) copy-start(bf16[2,128,128]{2,1,0:T(8,128)(2,1)} %out_weight.3) | copy-start | bytes 196612
  87.7 1.9 %collective-permute-start.1 = (bf16[128,16,128]{2,1,0:T(8,128)(2,1)S(1)}, bf16[128,16,128]{2,1,0:T(8,128)(2,1)S(1)}, u32[]{:S(2)}, u32[]{:S(2)}) collective-permute-start(bf16[128,16,128]{2,1,0:T(8,128)(2,1)S(1)} %all_to_all.22.own), channel_id=1, source_target_pairs={{0,16},{16,0},{32,48},{48,32},{64,80},{80,64},{96,112},{112,96},{1... | collective-permute-start | bytes 1572872 | tf_op jit(solution)/shard_map/ppermute | solution.py:31
  90.4 21.1 %copy-start.3 = (bf16[128,1024]{1,0:T(8,128)(2,1)S(1)}, bf16[128,1024]{1,0:T(8,128)(2,1)}, u32[]{:S(2)}) copy-start(bf16[128,1024]{1,0:T(8,128)(2,1)} %up.1) | copy-start | bytes 786436
  90.4 21.0 %copy-start.4 = (bf16[512,128]{1,0:T(8,128)(2,1)S(1)}, bf16[512,128]{1,0:T(8,128)(2,1)}, u32[]{:S(2)}) copy-start(bf16[512,128]{1,0:T(8,128)(2,1)} %down.1) | copy-start | bytes 393220

commit v5 on v4

--- a/solution.py
+++ b/solution.py
@@ -88,23 +88,10 @@
     factors[...] = scratch[...].reshape(WIDTH, 2 * STEPS, 128).astype(BF16)
 
 
-def first_kernel(
-    pair_hbm, gain_hbm, bias_hbm, weight_hbm, factors, pair, gain, bias, weight, scratch, sems
-):
-    sources = (weight_hbm.at[0], pair_hbm, gain_hbm, bias_hbm)
-    targets = (weight, pair, gain, bias)
-    copies = [
-        pltpu.make_async_copy(source, target, sems.at[i])
-        for i, (source, target) in enumerate(zip(sources, targets))
-    ]
-    for copy in copies:
-        copy.start()
-    for copy in copies:
-        copy.wait()
-    vectors = columns_of((gain, bias))
+def first_kernel(pair, norm_gain, norm_bias, weight, factors, scratch):
+    vectors = columns_of((norm_gain, norm_bias))
     normed = layer_norm(field_of(pair), vectors[:, 0:1], vectors[:, 3:4]).astype(BF16)
-    left, right = factors_of(dot(weight[:, : 4 * WIDTH].T, normed))
-    put_factors(scratch, left, right, factors)
+    put_factors(scratch, *factors_of(dot(weight[...], normed)), factors)
 
 
 def middle_kernel(
@@ -184,14 +171,27 @@
             product[rows] = tile.reshape(PAIRS, STEPS, 128).astype(BF16)
 
 
+def dot_rows(left, right):
+    return lax.dot_general(
+        left[...], right[...], (((1,), (1,)), ((), ())), preferred_element_type=F32
+    )
+
+
+def dot_columns(left, right):
+    return lax.dot_general(
+        left[...], right[...], (((0,), (0,)), ((), ())), preferred_element_type=F32
+    )
+
+
 def outgoing_own_kernel(
     own, pair, norm_gain, norm_bias, out_gain, out_bias, weight,
-    left, right, gates, fields, vectors,
+    left, own_product, gates, fields, vectors, right,
 ):
     for g in range(COLS // FOLD):
         columns = [g * FOLD + i for i in range(FOLD)]
         left[:, lanes_from(g)] = flat_rows(rows_of(own, columns, 0))
         right[:, lanes_from(g)] = flat_rows(rows_of(own, columns, 1))
+    send_product(dot_rows(left, right), own_product, range(PAIRS))
     vectors[...] = columns_of((norm_gain, norm_bias, out_gain, out_bias))
     field = field_of(pair)
     normed = layer_norm(field, vectors[:, 0:1], vectors[:, 3:4]).astype(BF16)
@@ -199,16 +199,15 @@
     fields[...] = field
 
 
-def outgoing_kernel(other, left, right_own, product, right):
+def outgoing_kernel(other, left, own_product, product, right):
     core = core_index()
     for g in range(COLS // FOLD):
         columns = [g * FOLD + i for i in range(FOLD)]
-        right[:, lanes_from(g)] = flat_rows(rows_of(other, columns, 1))
-    for factor, parity in ((right_own, core), (right, 1 - core)):
-        mixed = lax.dot_general(
-            left[...], factor[...], (((1,), (1,)), ((), ())), preferred_element_type=F32
-        )
-        send_product(mixed, product, [2 * a + parity for a in range(PAIRS)])
+        right[:, lanes_from(g)] = flat_rows(rows_of(other, columns, 0))
+    for a in range(PAIRS):
+        rows = pl.ds(member(0, 2 * a + core), PAIRS)
+        product[rows] = own_product[member(0, a) : member(0, a + 1)]
+    send_product(dot_rows(left, right), product, [2 * a + 1 - core for a in range(PAIRS)])
 
 
 def form_incoming(source, left, right):
@@ -221,19 +220,16 @@
         left[:, lanes_from(g)] = flat_rows(rows_of(source, columns, 0))
 
 
-def incoming_own_kernel(own, fields, vectors, weight, left, right, gates):
+def incoming_own_kernel(own, fields, vectors, weight, own_mixed, gates, left, right):
     form_incoming(own, left, right)
+    own_mixed[...] = dot_columns(left, right)
     normed = layer_norm(fields[...], vectors[:, 1:2], vectors[:, 4:5]).astype(BF16)
     gates[...] = sigmoid(dot(weight[1, :, 4 * WIDTH :].T, normed))
 
 
-def incoming_kernel(other, left_own, right_own, product, left, right):
+def incoming_kernel(other, own_mixed, product, left, right):
     form_incoming(other, left, right)
-    mixed = sum(
-        lax.dot_general(a[...], b[...], (((0,), (0,)), ((), ())), preferred_element_type=F32)
-        for a, b in ((left_own, right_own), (left, right))
-    )
-    send_product(mixed, product, range(COLS))
+    send_product(own_mixed[...] + dot_columns(left, right), product, range(COLS))
 
 
 def call(kernel, outs, scratch, name, vmem=40, **more):
@@ -262,34 +258,28 @@
     blocks = (FOLD, STEPS, SIDE, WIDTH)
 
     pair = pair.reshape(blocks)
-    operands = (pair, norm_gain, norm_bias)
-    landing = [pltpu.VMEM(v.shape, v.dtype) for v in operands]
-    landing += [pltpu.VMEM(proj_weight.shape[1:], BF16), packing, pltpu.SemaphoreType.DMA((4,))]
-    hbm = pl.BlockSpec(memory_space=pltpu.HBM)
-    factors = call(first_kernel, packed, landing, "first", 60, in_specs=[hbm] * 4)(
-        *operands, proj_weight
+    factors = call(first_kernel, packed, [packing], "first")(
+        pair, norm_gain, norm_bias, proj_weight[0, :, : 4 * WIDTH].T
+    )
+    own = exchange(factors)
+    other = swap_cores(own[:, STEPS:])
+    wide, square = (HALF, FULL), (HALF, HALF)
+    outs = (shape(*wide), shape(WIDTH // 2, STEPS, 128), flat, flat)
+    factor, square = pltpu.VMEM(wide, BF16), pltpu.VMEM(square, BF16)
+    left, own_product, gate, field, vectors = call(
+        outgoing_own_kernel, (*outs, shape(WIDTH, WIDTH, dtype=F32)), [factor], "outgoing_own"
+    )(own, pair, norm_gain, norm_bias, out_gain, out_bias, proj_weight)
+    mixed = call(outgoing_kernel, product, [factor], "outgoing")(other, left, own_product)
+    factors, field = call(middle_kernel, (packed, flat), [packing, unpacking], "middle")(
+        exchange(mixed), gate, field, vectors, proj_weight, out_weight
     )
     own = exchange(factors)
     other = swap_cores(own)
-    wide, square = (HALF, FULL), (HALF, HALF)
-    outs = (shape(*wide), shape(*wide), flat, flat, shape(WIDTH, WIDTH, dtype=F32))
-    left, right, gate, field, vectors = call(outgoing_own_kernel, outs, [], "outgoing_own")(
-        own, pair, norm_gain, norm_bias, out_gain, out_bias, proj_weight
-    )
-    mixed = call(outgoing_kernel, product, [pltpu.VMEM(wide, BF16)], "outgoing")(
-        other, left, right
-    )
-    factors, field = call(middle_kernel, (packed, flat), [packing, unpacking], "middle")(
-        exchange(mixed), gate, field, vectors, proj_weight, out_weight
-    )
-    own = exchange(factors)
-    other = swap_cores(own)
-    outs = (shape(*square), shape(*wide), flat)
-    left, right, gate = call(incoming_own_kernel, outs, [], "incoming_own")(
+    outs = (shape(*wide, dtype=F32), flat)
+    own_mixed, gate = call(incoming_own_kernel, outs, [square, factor], "incoming_own")(
         own, field, vectors, proj_weight
     )
-    forming = [pltpu.VMEM(square, BF16), pltpu.VMEM(wide, BF16)]
-    mixed = call(incoming_kernel, product, forming, "incoming")(other, left, right)
+    mixed = call(incoming_kernel, product, [square, factor], "incoming")(other, own_mixed)
     updated = call(last_kernel, shape(*blocks), [unpacking], "last")(
         exchange(mixed), gate, field, vectors, out_weight, up_weight, down_weight
     )

time: 114 us -> 113 us (level)
  local copies, waits for them, and re-layouts: 0.06 us -> 2.64 us
  Pallas kernels: 9.42 us -> 7.56 us
    pallas_call x5, Pallas kernels: 6.16 us -> 4.29 us  [the longest x1 1.3 us: body(): call(outgoing_own_kernel, (*outs, shape(WIDTH, WIDTH, dtype=F32)), [facto...]
    unnamed x18 -> x19, local copies, waits for them, and re-layouts: 0.06 us -> 1.67 us
  transfers between devices with their start and end apart: 2 -> 2, of which waited for: 2 -> 1; matrix products, arithmetic and copies ran while one was open for 0% -> 0% of each run, Pallas kernels for 2% -> 2%
where the time goes in v5:
time: 113 us
  blocking collectives  101 us (89%)
  Pallas kernels  7.56 us (7%)
  local copies, waits for them, and re-layouts  2.64 us (2%)
  waiting for transfers between devices  1.25 us (1%)
    all_to_all x4, blocking collectives, exchange(): lax.all_to_all(values, ('row', 'col'), 0, 0, axis_index_groups=PARITY)  101 us
  transfers between devices with their start and end apart: 2, of which 1 were waited for; matrix products, arithmetic and copies ran while one was open for 0% of the time, Pallas kernels for 2%

profile of v5, /device:TPU:2, one launch (start us, length us, event | category | flops | bytes accessed | tf_op | source)
XLA Modules:
  0.0 112.7 jit_solution(9664378292381194323)
XLA Ops:
  0.0 0.0 copy-start.1
  0.0 1.0 slice.6
  1.0 0.0 copy-start.6
  1.0 0.1 copy.11
  1.1 0.0 copy-start.5
  1.1 0.0 copy-done.1
  1.1 0.5 copy-done.6
  1.7 0.1 copy-done.5
  1.8 0.9 first.1
  2.7 34.7 %all_to_all.20.own = bf16[128,16,128]{2,1,0:T(8,128)(2,1)S(1)} all-to-all(bf16[128,16,128]{2,1,0:T(8,128)(2,1)S(1)} %first.1), channel_id=1, replica_groups={{0,32,64,96,128,160,192,224,1,33,65,97,129,161,193,225,2,34,66,98,130,1..., dimensions={0} | all-to-all | bytes 1048576 | tf_op jit(solution)/shard_map/all_to_all | solution.py:27
  37.5 0.1 collective-permute-start
  37.6 0.8 copy-done
  38.4 0.0 copy-done.7
  38.4 0.0 copy-done.8
  38.4 1.3 %outgoing_own.1 = (bf16[256,512]{1,0:T(8,128)(2,1)S(1)}, bf16[64,8,128]{2,1,0:T(8,128)(2,1)S(1)}, f32[128,1024]{1,0:T(8,128)S(1)}, f32[128,1024]{1,0:T(8,128)S(1)}, f32[128,128]{1,0:T(8,128)S(1)}) custom-call(bf16[128,16,128]{2,1,0:T(8,128)(2,1)S(1)} %all_to_all.20.own, bf16[4,8,32,128]{3,2,1,0:T(8,128)(2,1)S(1)} %bitcast.6, f32[3,128]{1,0:T(4,128)S(1)} %copy-done.5, ...), custom_call_target="tpu_custom_call" | custom-call | tf_op jit(solution)/shard_map/outgoing_own/pallas_call | solution.py:269
  39.7 0.0 collective-permute-done.other
  39.7 0.6 outgoing.1
  40.4 0.0 copy-start.2
  40.4 20.4 %all_to_all.21.mixed = bf16[128,8,128]{2,1,0:T(8,128)(2,1)S(1)} all-to-all(bf16[128,8,128]{2,1,0:T(8,128)(2,1)S(1)} %outgoing.1), channel_id=1, replica_groups={{0,32,64,96,128,160,192,224,1,33,65,97,129,161,193,225,2,34,66,98,130,1..., dimensions={0} | all-to-all | bytes 524288 | tf_op jit(solution)/shard_map/all_to_all | solution.py:27
  60.7 0.0 copy-done.2
  60.7 1.1 middle.1
  61.9 24.9 %all_to_all.22.own = bf16[128,16,128]{2,1,0:T(8,128)(2,1)S(1)} all-to-all(bf16[128,16,128]{2,1,0:T(8,128)(2,1)S(1)} %get-tuple-element.19), channel_id=1, replica_groups={{0,32,64,96,128,160,192,224,1,33,65,97,129,161,193,225,2,34,66,98,130,1..., dimensions={0} | all-to-all | bytes 1048576 | tf_op jit(solution)/shard_map/all_to_all | solution.py:27
  86.7 0.0 collective-permute-start.1
  86.7 0.7 incoming_own.1
  87.4 1.2 %collective-permute-done.1.other = bf16[128,16,128]{2,1,0:T(8,128)(2,1)S(1)} collective-permute-done((bf16[128,16,128]{2,1,0:T(8,128)(2,1)S(1)}, bf16[128,16,128]{2,1,0:T(8,128)(2,1)S(1)}, u32[]{:S(2)}, u32[]{:S(2)}) %collective-permute-start.1) | collective-permute-done | bytes 524320 | tf_op jit(solution)/shard_map/ppermute | solution.py:31
  88.6 0.8 incoming.1
  89.5 0.0 copy-start.3
  89.5 0.0 copy-start.4
  89.5 21.0 %all_to_all.23.mixed = bf16[128,8,128]{2,1,0:T(8,128)(2,1)S(1)} all-to-all(bf16[128,8,128]{2,1,0:T(8,128)(2,1)S(1)} %incoming.1), channel_id=1, replica_groups={{0,32,64,96,128,160,192,224,1,33,65,97,129,161,193,225,2,34,66,98,130,1..., dimensions={0} | all-to-all | bytes 524288 | tf_op jit(solution)/shard_map/all_to_all | solution.py:27
  110.5 0.0 copy-done.3
  110.5 0.0 copy-done.4
  110.5 2.1 %last.1 = bf16[4,8,32,128]{3,2,1,0:T(8,128)(2,1)} custom-call(bf16[128,8,128]{2,1,0:T(8,128)(2,1)S(1)} %all_to_all.23.mixed, f32[128,1024]{1,0:T(8,128)S(1)} %get-tuple-element.22.gates, f32[128,1024]{1,0:T(8,128)S(1)} %get-tuple-element.20.fields, f32[128,128]{1,0:T(8,128)S(1)} %get-tuple-element.18.vectors, bf16[2,128,128]{2,1,0:T(8,128)(2,1)S(1)} %copy-done.2, ...), custom_call_target="tpu_custom_call" | custom-call | tf_op jit(solution)/shard_map/last/pallas_call | solution.py:283
  (4 shorter events, 0.0 us)
Async XLA Ops:
  0.0 1.1 copy-start.1
  1.0 0.7 copy-start.6
  1.1 0.7 copy-start.5
  37.4 1.0 copy-start
  37.4 1.0 copy-start.7
  37.5 1.0 copy-start.8
  37.5 2.3 %collective-permute-start = (bf16[128,8,128]{2,1,0:T(8,128)(2,1)S(1)}, bf16[128,8,128]{2,1,0:T(8,128)(2,1)S(1)}, u32[]{:S(2)}, u32[]{:S(2)}) collective-permute-start(bf16[128,8,128]{2,1,0:T(8,128)(2,1)S(1)} %slice.8), channel_id=1, source_target_pairs={{0,16},{16,0},{32,48},{48,32},{64,80},{80,64},{96,112},{112,96},{1... | collective-permute-start | bytes 786440 | tf_op jit(solution)/shard_map/ppermute | solution.py:31
  40.4 20.4 %copy-start.2 = (bf16[2,128,128]{2,1,0:T(8,128)(2,1)S(1)}, bf16[2,128,128]{2,1,0:T(8,128)(2,1)}, u32[]{:S(2)}) copy-start(bf16[2,128,128]{2,1,0:T(8,128)(2,1)} %out_weight.3) | copy-start | bytes 196612
  86.7 1.9 %collective-permute-start.1 = (bf16[128,16,128]{2,1,0:T(8,128)(2,1)S(1)}, bf16[128,16,128]{2,1,0:T(8,128)(2,1)S(1)}, u32[]{:S(2)}, u32[]{:S(2)}) collective-permute-start(bf16[128,16,128]{2,1,0:T(8,128)(2,1)S(1)} %all_to_all.22.own), channel_id=1, source_target_pairs={{0,16},{16,0},{32,48},{48,32},{64,80},{80,64},{96,112},{112,96},{1... | collective-permute-start | bytes 1572872 | tf_op jit(solution)/shard_map/ppermute | solution.py:31
  89.5 21.1 %copy-start.3 = (bf16[128,1024]{1,0:T(8,128)(2,1)S(1)}, bf16[128,1024]{1,0:T(8,128)(2,1)}, u32[]{:S(2)}) copy-start(bf16[128,1024]{1,0:T(8,128)(2,1)} %up.1) | copy-start | bytes 786436
  89.5 21.0 %copy-start.4 = (bf16[512,128]{1,0:T(8,128)(2,1)S(1)}, bf16[512,128]{1,0:T(8,128)(2,1)}, u32[]{:S(2)}) copy-start(bf16[512,128]{1,0:T(8,128)(2,1)} %down.1) | copy-start | bytes 393220

commit v6 on v5

--- a/solution.py
+++ b/solution.py
@@ -35,8 +35,16 @@
     return lax.rem(lax.axis_index("row"), 2)
 
 
-def sigmoid(x):
-    return 0.5 + 0.5 * jnp.tanh(0.5 * x)
+def halved(weight):
+    return weight * jnp.asarray(0.5, weight.dtype)
+
+
+def sigmoid_of_double(half):
+    return 0.5 + 0.5 * jnp.tanh(half)
+
+
+def times_sigmoid_of_double(half, other):
+    return other * jnp.tanh(half) + other
 
 
 def layer_norm(values, gain, bias):
@@ -56,7 +64,7 @@
 
 
 def take_mixed(mixed, scratch):
-    scratch[...] = mixed[...].astype(F32).reshape(WIDTH * STEPS, 128)
+    scratch[: WIDTH * STEPS] = mixed[...].astype(F32).reshape(WIDTH * STEPS, 128)
     steps = [scratch[pl.ds(step, WIDTH, stride=STEPS), :] for step in range(STEPS)]
     return jnp.concatenate(steps, axis=1)
 
@@ -75,8 +83,8 @@
 
 def factors_of(proj):
     h = WIDTH
-    left = sigmoid(proj[:h]) * proj[h : 2 * h]
-    right = sigmoid(proj[2 * h : 3 * h]) * proj[3 * h : 4 * h]
+    left = times_sigmoid_of_double(proj[:h], proj[h : 2 * h])
+    right = times_sigmoid_of_double(proj[2 * h : 3 * h], proj[3 * h : 4 * h])
     return left, right
 
 
@@ -85,13 +93,14 @@
         lanes = slice(step * 128, (step + 1) * 128)
         scratch[pl.ds(step, WIDTH, stride=2 * STEPS), :] = left[:, lanes]
         scratch[pl.ds(step + STEPS, WIDTH, stride=2 * STEPS), :] = right[:, lanes]
-    factors[...] = scratch[...].reshape(WIDTH, 2 * STEPS, 128).astype(BF16)
+    rows = scratch[: WIDTH * 2 * STEPS]
+    factors[...] = rows.reshape(WIDTH, 2 * STEPS, 128).astype(BF16)
 
 
 def first_kernel(pair, norm_gain, norm_bias, weight, factors, scratch):
     vectors = columns_of((norm_gain, norm_bias))
     normed = layer_norm(field_of(pair), vectors[:, 0:1], vectors[:, 3:4]).astype(BF16)
-    put_factors(scratch, *factors_of(dot(weight[...], normed)), factors)
+    put_factors(scratch, *factors_of(dot(halved(weight[...]), normed)), factors)
 
 
 def middle_kernel(
@@ -103,7 +112,7 @@
         fields[...], take_mixed(mixed, product), mix_gain, mix_bias, out_weight[0].T, gates[...]
     )
     normed = layer_norm(field, gain, bias).astype(BF16)
-    put_factors(scratch, *factors_of(dot(weight[1, :, : 4 * WIDTH].T, normed)), factors)
+    put_factors(scratch, *factors_of(dot(halved(weight[1, :, : 4 * WIDTH]).T, normed)), factors)
     fields_out[...] = field
 
 
@@ -114,9 +123,9 @@
     field = finish(
         fields[...], take_mixed(mixed, product), mix_gain, mix_bias, out_weight[1].T, gates[...]
     )
-    expanded = dot(up[...].T, layer_norm(field, gain, bias).astype(BF16))
-    wide = expanded[:inner]
-    act = (wide * sigmoid(wide) * expanded[inner:]).astype(BF16)
+    tnorm = layer_norm(field, gain, bias).astype(BF16)
+    half = dot(halved(up[:, :inner]).T, tnorm)
+    act = (times_sigmoid_of_double(half, half) * dot(up[:, inner:].T, tnorm)).astype(BF16)
     field = field + dot(down[...].T, act)
     for i in range(STEPS):
         block = field[:, i * 128 : (i + 1) * 128].T.reshape(FOLD, SIDE, WIDTH)
@@ -195,7 +204,7 @@
     vectors[...] = columns_of((norm_gain, norm_bias, out_gain, out_bias))
     field = field_of(pair)
     normed = layer_norm(field, vectors[:, 0:1], vectors[:, 3:4]).astype(BF16)
-    gates[...] = sigmoid(dot(weight[0, :, 4 * WIDTH :].T, normed))
+    gates[...] = sigmoid_of_double(dot(halved(weight[0, :, 4 * WIDTH :]).T, normed))
     fields[...] = field
 
 
@@ -224,7 +233,7 @@
     form_incoming(own, left, right)
     own_mixed[...] = dot_columns(left, right)
     normed = layer_norm(fields[...], vectors[:, 1:2], vectors[:, 4:5]).astype(BF16)
-    gates[...] = sigmoid(dot(weight[1, :, 4 * WIDTH :].T, normed))
+    gates[...] = sigmoid_of_double(dot(halved(weight[1, :, 4 * WIDTH :]).T, normed))
 
 
 def incoming_kernel(other, own_mixed, product, left, right):
@@ -253,8 +262,8 @@
     flat = shape(WIDTH, STEPS * 128, dtype=F32)
     packed = shape(WIDTH, 2 * STEPS, 128)
     product = shape(WIDTH, STEPS, 128)
-    packing = pltpu.VMEM((WIDTH * 2 * STEPS, 128), F32)
-    unpacking = pltpu.VMEM((WIDTH * STEPS, 128), F32)
+    packing = pltpu.VMEM(((WIDTH + 1) * 2 * STEPS, 128), F32)
+    unpacking = pltpu.VMEM(((WIDTH + 1) * STEPS, 128), F32)
     blocks = (FOLD, STEPS, SIDE, WIDTH)
 
     pair = pair.reshape(blocks)

time: 113 us -> 113 us (level)
  no operation moved by 1% of the time
where the time goes in v6:
time: 113 us
  blocking collectives  101 us (89%)
  Pallas kernels  7.49 us (7%)
  local copies, waits for them, and re-layouts  2.64 us (2%)
  waiting for transfers between devices  1.23 us (1%)
    all_to_all x4, blocking collectives, exchange(): lax.all_to_all(values, ('row', 'col'), 0, 0, axis_index_groups=PARITY)  101 us
  transfers between devices with their start and end apart: 2, of which 1 were waited for; matrix products, arithmetic and copies ran while one was open for 0% of the time, Pallas kernels for 2%

profile of v6, /device:TPU:2, one launch (start us, length us, event | category | flops | bytes accessed | tf_op | source)
XLA Modules:
  0.0 112.6 jit_solution(16744796974488889877)
XLA Ops:
  0.0 0.0 copy-start.1
  0.0 1.0 slice.6
  1.0 0.0 copy-start.6
  1.0 0.1 copy.11
  1.1 0.0 copy-start.5
  1.1 0.0 copy-done.1
  1.1 0.5 copy-done.6
  1.7 0.1 copy-done.5
  1.8 0.9 first.1
  2.7 34.7 %all_to_all.20.own = bf16[128,16,128]{2,1,0:T(8,128)(2,1)S(1)} all-to-all(bf16[128,16,128]{2,1,0:T(8,128)(2,1)S(1)} %first.1), channel_id=1, replica_groups={{0,32,64,96,128,160,192,224,1,33,65,97,129,161,193,225,2,34,66,98,130,1..., dimensions={0} | all-to-all | bytes 1048576 | tf_op jit(solution)/shard_map/all_to_all | solution.py:27
  37.4 0.1 collective-permute-start
  37.5 0.8 copy-done
  38.4 0.0 copy-done.7
  38.4 0.0 copy-done.8
  38.4 1.3 %outgoing_own.1 = (bf16[256,512]{1,0:T(8,128)(2,1)S(1)}, bf16[64,8,128]{2,1,0:T(8,128)(2,1)S(1)}, f32[128,1024]{1,0:T(8,128)S(1)}, f32[128,1024]{1,0:T(8,128)S(1)}, f32[128,128]{1,0:T(8,128)S(1)}) custom-call(bf16[128,16,128]{2,1,0:T(8,128)(2,1)S(1)} %all_to_all.20.own, bf16[4,8,32,128]{3,2,1,0:T(8,128)(2,1)S(1)} %bitcast.6, f32[3,128]{1,0:T(4,128)S(1)} %copy-done.5, ...), custom_call_target="tpu_custom_call" | custom-call | tf_op jit(solution)/shard_map/outgoing_own/pallas_call | solution.py:278
  39.7 0.0 collective-permute-done.other
  39.7 0.6 outgoing.1
  40.3 0.0 copy-start.2
  40.3 20.4 %all_to_all.21.mixed = bf16[128,8,128]{2,1,0:T(8,128)(2,1)S(1)} all-to-all(bf16[128,8,128]{2,1,0:T(8,128)(2,1)S(1)} %outgoing.1), channel_id=1, replica_groups={{0,32,64,96,128,160,192,224,1,33,65,97,129,161,193,225,2,34,66,98,130,1..., dimensions={0} | all-to-all | bytes 524288 | tf_op jit(solution)/shard_map/all_to_all | solution.py:27
  60.7 0.0 copy-done.2
  60.7 1.1 middle.1
  61.8 24.9 %all_to_all.22.own = bf16[128,16,128]{2,1,0:T(8,128)(2,1)S(1)} all-to-all(bf16[128,16,128]{2,1,0:T(8,128)(2,1)S(1)} %get-tuple-element.19), channel_id=1, replica_groups={{0,32,64,96,128,160,192,224,1,33,65,97,129,161,193,225,2,34,66,98,130,1..., dimensions={0} | all-to-all | bytes 1048576 | tf_op jit(solution)/shard_map/all_to_all | solution.py:27
  86.6 0.0 collective-permute-start.1
  86.6 0.7 incoming_own.1
  87.3 1.2 %collective-permute-done.1.other = bf16[128,16,128]{2,1,0:T(8,128)(2,1)S(1)} collective-permute-done((bf16[128,16,128]{2,1,0:T(8,128)(2,1)S(1)}, bf16[128,16,128]{2,1,0:T(8,128)(2,1)S(1)}, u32[]{:S(2)}, u32[]{:S(2)}) %collective-permute-start.1) | collective-permute-done | bytes 524320 | tf_op jit(solution)/shard_map/ppermute | solution.py:31
  88.5 0.8 incoming.1
  89.4 0.0 copy-start.3
  89.4 0.0 copy-start.4
  89.4 21.0 %all_to_all.23.mixed = bf16[128,8,128]{2,1,0:T(8,128)(2,1)S(1)} all-to-all(bf16[128,8,128]{2,1,0:T(8,128)(2,1)S(1)} %incoming.1), channel_id=1, replica_groups={{0,32,64,96,128,160,192,224,1,33,65,97,129,161,193,225,2,34,66,98,130,1..., dimensions={0} | all-to-all | bytes 524288 | tf_op jit(solution)/shard_map/all_to_all | solution.py:27
  110.4 0.0 copy-done.3
  110.4 0.0 copy-done.4
  110.4 2.1 %last.1 = bf16[4,8,32,128]{3,2,1,0:T(8,128)(2,1)} custom-call(bf16[128,8,128]{2,1,0:T(8,128)(2,1)S(1)} %all_to_all.23.mixed, f32[128,1024]{1,0:T(8,128)S(1)} %get-tuple-element.22.gates, f32[128,1024]{1,0:T(8,128)S(1)} %get-tuple-element.20.fields, f32[128,128]{1,0:T(8,128)S(1)} %get-tuple-element.18.vectors, bf16[2,128,128]{2,1,0:T(8,128)(2,1)S(1)} %copy-done.2, ...), custom_call_target="tpu_custom_call" | custom-call | tf_op jit(solution)/shard_map/last/pallas_call | solution.py:292
  (4 shorter events, 0.0 us)
Async XLA Ops:
  0.0 1.1 copy-start.1
  1.0 0.7 copy-start.6
  1.1 0.7 copy-start.5
  37.4 1.0 copy-start
  37.4 1.0 copy-start.7
  37.4 1.0 copy-start.8
  37.4 2.3 %collective-permute-start = (bf16[128,8,128]{2,1,0:T(8,128)(2,1)S(1)}, bf16[128,8,128]{2,1,0:T(8,128)(2,1)S(1)}, u32[]{:S(2)}, u32[]{:S(2)}) collective-permute-start(bf16[128,8,128]{2,1,0:T(8,128)(2,1)S(1)} %slice.8), channel_id=1, source_target_pairs={{0,16},{16,0},{32,48},{48,32},{64,80},{80,64},{96,112},{112,96},{1... | collective-permute-start | bytes 786440 | tf_op jit(solution)/shard_map/ppermute | solution.py:31
  40.3 20.4 %copy-start.2 = (bf16[2,128,128]{2,1,0:T(8,128)(2,1)S(1)}, bf16[2,128,128]{2,1,0:T(8,128)(2,1)}, u32[]{:S(2)}) copy-start(bf16[2,128,128]{2,1,0:T(8,128)(2,1)} %out_weight.3) | copy-start | bytes 196612
  86.6 1.9 %collective-permute-start.1 = (bf16[128,16,128]{2,1,0:T(8,128)(2,1)S(1)}, bf16[128,16,128]{2,1,0:T(8,128)(2,1)S(1)}, u32[]{:S(2)}, u32[]{:S(2)}) collective-permute-start(bf16[128,16,128]{2,1,0:T(8,128)(2,1)S(1)} %all_to_all.22.own), channel_id=1, source_target_pairs={{0,16},{16,0},{32,48},{48,32},{64,80},{80,64},{96,112},{112,96},{1... | collective-permute-start | bytes 1572872 | tf_op jit(solution)/shard_map/ppermute | solution.py:31
  89.4 21.1 %copy-start.3 = (bf16[128,1024]{1,0:T(8,128)(2,1)S(1)}, bf16[128,1024]{1,0:T(8,128)(2,1)}, u32[]{:S(2)}) copy-start(bf16[128,1024]{1,0:T(8,128)(2,1)} %up.1) | copy-start | bytes 786436
  89.4 21.0 %copy-start.4 = (bf16[512,128]{1,0:T(8,128)(2,1)S(1)}, bf16[512,128]{1,0:T(8,128)(2,1)}, u32[]{:S(2)}) copy-start(bf16[512,128]{1,0:T(8,128)(2,1)} %down.1) | copy-start | bytes 393220

commit v7 on v6

--- a/solution.py
+++ b/solution.py
@@ -100,7 +100,7 @@
 def first_kernel(pair, norm_gain, norm_bias, weight, factors, scratch):
     vectors = columns_of((norm_gain, norm_bias))
     normed = layer_norm(field_of(pair), vectors[:, 0:1], vectors[:, 3:4]).astype(BF16)
-    put_factors(scratch, *factors_of(dot(halved(weight[...]), normed)), factors)
+    put_factors(scratch, *factors_of(dot(halved(weight[: 4 * WIDTH]), normed)), factors)
 
 
 def middle_kernel(
@@ -159,11 +159,9 @@
 
 def rows_of(source, columns, half):
     rows = slice(half * STEPS, (half + 1) * STEPS)
-    tiles = [
-        source[pl.ds(member(0, q), PAIRS), rows, :].astype(F32).reshape(PAIRS * STEPS, 128)
-        for q in columns
-    ]
-    tiles = [tile.reshape(PAIRS, 1, STEPS, 128) for tile in turn(tiles)]
+    tiles = [source[pl.ds(member(0, q), PAIRS)].astype(F32)[:, rows] for q in columns]
+    tiles = turn([tile.reshape(PAIRS * STEPS, 128) for tile in tiles])
+    tiles = [tile.reshape(PAIRS, 1, STEPS, 128) for tile in tiles]
     return jnp.concatenate(tiles, axis=1)
 
 
@@ -204,7 +202,7 @@
     vectors[...] = columns_of((norm_gain, norm_bias, out_gain, out_bias))
     field = field_of(pair)
     normed = layer_norm(field, vectors[:, 0:1], vectors[:, 3:4]).astype(BF16)
-    gates[...] = sigmoid_of_double(dot(halved(weight[0, :, 4 * WIDTH :]).T, normed))
+    gates[...] = sigmoid_of_double(dot(halved(weight[4 * WIDTH :]), normed))
     fields[...] = field
 
 
@@ -267,8 +265,9 @@
     blocks = (FOLD, STEPS, SIDE, WIDTH)
 
     pair = pair.reshape(blocks)
+    first_weight = proj_weight[0].T
     factors = call(first_kernel, packed, [packing], "first")(
-        pair, norm_gain, norm_bias, proj_weight[0, :, : 4 * WIDTH].T
+        pair, norm_gain, norm_bias, first_weight
     )
     own = exchange(factors)
     other = swap_cores(own[:, STEPS:])
@@ -277,7 +276,7 @@
     factor, square = pltpu.VMEM(wide, BF16), pltpu.VMEM(square, BF16)
     left, own_product, gate, field, vectors = call(
         outgoing_own_kernel, (*outs, shape(WIDTH, WIDTH, dtype=F32)), [factor], "outgoing_own"
-    )(own, pair, norm_gain, norm_bias, out_gain, out_bias, proj_weight)
+    )(own, pair, norm_gain, norm_bias, out_gain, out_bias, first_weight)
     mixed = call(outgoing_kernel, product, [factor], "outgoing")(other, left, own_product)
     factors, field = call(middle_kernel, (packed, flat), [packing, unpacking], "middle")(
         exchange(mixed), gate, field, vectors, proj_weight, out_weight

time: 113 us -> 113 us (level)
  no operation moved by 1% of the time
where the time goes in v7:
time: 113 us
  blocking collectives  101 us (89%)
  Pallas kernels  7.37 us (7%)
  local copies, waits for them, and re-layouts  2.37 us (2%)
  waiting for transfers between devices  1.24 us (1%)
    all_to_all x4, blocking collectives, exchange(): lax.all_to_all(values, ('row', 'col'), 0, 0, axis_index_groups=PARITY)  101 us
  transfers between devices with their start and end apart: 2, of which 1 were waited for; matrix products, arithmetic and copies ran while one was open for 0% of the time, Pallas kernels for 2%

profile of v7, /device:TPU:2, one launch (start us, length us, event | category | flops | bytes accessed | tf_op | source)
XLA Modules:
  0.0 112.6 jit_solution(9590498604191068674)
XLA Ops:
  0.0 0.0 slice-start
  0.0 0.0 copy-start.1
  0.0 0.9 slice-done
  0.9 0.2 copy.11
  1.1 0.0 copy-done.1
  1.1 0.5 copy-done.6
  1.6 0.2 copy-done.5
  1.8 0.9 first.1
  2.7 34.7 %all_to_all.20.own = bf16[128,16,128]{2,1,0:T(8,128)(2,1)S(1)} all-to-all(bf16[128,16,128]{2,1,0:T(8,128)(2,1)S(1)} %first.1), channel_id=1, replica_groups={{0,32,64,96,128,160,192,224,1,33,65,97,129,161,193,225,2,34,66,98,130,1..., dimensions={0} | all-to-all | bytes 1048576 | tf_op jit(solution)/shard_map/all_to_all | solution.py:27
  37.4 0.1 collective-permute-start
  37.5 0.6 copy-done.7
  38.1 0.0 copy-done.8
  38.1 1.2 %outgoing_own.1 = (bf16[256,512]{1,0:T(8,128)(2,1)S(1)}, bf16[64,8,128]{2,1,0:T(8,128)(2,1)S(1)}, f32[128,1024]{1,0:T(8,128)S(1)}, f32[128,1024]{1,0:T(8,128)S(1)}, f32[128,128]{1,0:T(8,128)S(1)}) custom-call(bf16[128,16,128]{2,1,0:T(8,128)(2,1)S(1)} %all_to_all.20.own, bf16[4,8,32,128]{3,2,1,0:T(8,128)(2,1)S(1)} %bitcast.8, f32[3,128]{1,0:T(4,128)S(1)} %copy-done.5, ...), custom_call_target="tpu_custom_call" | custom-call | tf_op jit(solution)/shard_map/outgoing_own/pallas_call | solution.py:277
  39.3 0.0 collective-permute-done.other
  39.3 0.6 outgoing.1
  39.9 0.0 copy-start
  39.9 0.0 copy-start.2
  39.9 20.6 %all_to_all.21.mixed = bf16[128,8,128]{2,1,0:T(8,128)(2,1)S(1)} all-to-all(bf16[128,8,128]{2,1,0:T(8,128)(2,1)S(1)} %outgoing.1), channel_id=1, replica_groups={{0,32,64,96,128,160,192,224,1,33,65,97,129,161,193,225,2,34,66,98,130,1..., dimensions={0} | all-to-all | bytes 524288 | tf_op jit(solution)/shard_map/all_to_all | solution.py:27
  60.5 0.0 copy-done
  60.5 0.0 copy-done.2
  60.5 1.1 middle.1
  61.6 25.0 %all_to_all.22.own = bf16[128,16,128]{2,1,0:T(8,128)(2,1)S(1)} all-to-all(bf16[128,16,128]{2,1,0:T(8,128)(2,1)S(1)} %get-tuple-element.19), channel_id=1, replica_groups={{0,32,64,96,128,160,192,224,1,33,65,97,129,161,193,225,2,34,66,98,130,1..., dimensions={0} | all-to-all | bytes 1048576 | tf_op jit(solution)/shard_map/all_to_all | solution.py:27
  86.6 0.0 collective-permute-start.1
  86.6 0.7 incoming_own.1
  87.3 1.2 %collective-permute-done.1.other = bf16[128,16,128]{2,1,0:T(8,128)(2,1)S(1)} collective-permute-done((bf16[128,16,128]{2,1,0:T(8,128)(2,1)S(1)}, bf16[128,16,128]{2,1,0:T(8,128)(2,1)S(1)}, u32[]{:S(2)}, u32[]{:S(2)}) %collective-permute-start.1) | collective-permute-done | bytes 524320 | tf_op jit(solution)/shard_map/ppermute | solution.py:31
  88.5 0.8 incoming.1
  89.4 0.0 copy-start.3
  89.4 0.0 copy-start.4
  89.4 21.0 %all_to_all.23.mixed = bf16[128,8,128]{2,1,0:T(8,128)(2,1)S(1)} all-to-all(bf16[128,8,128]{2,1,0:T(8,128)(2,1)S(1)} %incoming.1), channel_id=1, replica_groups={{0,32,64,96,128,160,192,224,1,33,65,97,129,161,193,225,2,34,66,98,130,1..., dimensions={0} | all-to-all | bytes 524288 | tf_op jit(solution)/shard_map/all_to_all | solution.py:27
  110.4 0.0 copy-done.3
  110.4 0.0 copy-done.4
  110.4 2.1 %last.1 = bf16[4,8,32,128]{3,2,1,0:T(8,128)(2,1)} custom-call(bf16[128,8,128]{2,1,0:T(8,128)(2,1)S(1)} %all_to_all.23.mixed, f32[128,1024]{1,0:T(8,128)S(1)} %get-tuple-element.22.gates, f32[128,1024]{1,0:T(8,128)S(1)} %get-tuple-element.20.fields, f32[128,128]{1,0:T(8,128)S(1)} %get-tuple-element.18.vectors, bf16[2,128,128]{2,1,0:T(8,128)(2,1)S(1)} %copy-done.2, ...), custom_call_target="tpu_custom_call" | custom-call | tf_op jit(solution)/shard_map/last/pallas_call | solution.py:291
  (5 shorter events, 0.0 us)
Async XLA Ops:
  0.0 0.9 slice-start
  0.0 1.1 copy-start.1
  0.9 0.7 copy-start.6
  1.1 0.7 copy-start.5
  37.4 0.7 copy-start.7
  37.4 0.7 copy-start.8
  37.4 1.8 %collective-permute-start = (bf16[128,8,128]{2,1,0:T(8,128)(2,1)S(1)}, bf16[128,8,128]{2,1,0:T(8,128)(2,1)S(1)}, u32[]{:S(2)}, u32[]{:S(2)}) collective-permute-start(bf16[128,8,128]{2,1,0:T(8,128)(2,1)S(1)} %slice.8), channel_id=1, source_target_pairs={{0,16},{16,0},{32,48},{48,32},{64,80},{80,64},{96,112},{112,96},{1... | collective-permute-start | bytes 786440 | tf_op jit(solution)/shard_map/ppermute | solution.py:31
  39.9 20.7 %copy-start = (bf16[2,128,640]{2,1,0:T(8,128)(2,1)S(1)}, bf16[2,128,640]{2,1,0:T(8,128)(2,1)}, u32[]{:S(2)}) copy-start(bf16[2,128,640]{2,1,0:T(8,128)(2,1)} %weight.3) | copy-start | bytes 983044
  39.9 20.7 %copy-start.2 = (bf16[2,128,128]{2,1,0:T(8,128)(2,1)S(1)}, bf16[2,128,128]{2,1,0:T(8,128)(2,1)}, u32[]{:S(2)}) copy-start(bf16[2,128,128]{2,1,0:T(8,128)(2,1)} %out_weight.3) | copy-start | bytes 196612
  86.6 1.9 %collective-permute-start.1 = (bf16[128,16,128]{2,1,0:T(8,128)(2,1)S(1)}, bf16[128,16,128]{2,1,0:T(8,128)(2,1)S(1)}, u32[]{:S(2)}, u32[]{:S(2)}) collective-permute-start(bf16[128,16,128]{2,1,0:T(8,128)(2,1)S(1)} %all_to_all.22.own), channel_id=1, source_target_pairs={{0,16},{16,0},{32,48},{48,32},{64,80},{80,64},{96,112},{112,96},{1... | collective-permute-start | bytes 1572872 | tf_op jit(solution)/shard_map/ppermute | solution.py:31
  89.4 21.0 %copy-start.3 = (bf16[128,1024]{1,0:T(8,128)(2,1)S(1)}, bf16[128,1024]{1,0:T(8,128)(2,1)}, u32[]{:S(2)}) copy-start(bf16[128,1024]{1,0:T(8,128)(2,1)} %up.1) | copy-start | bytes 786436
  89.4 21.0 %copy-start.4 = (bf16[512,128]{1,0:T(8,128)(2,1)S(1)}, bf16[512,128]{1,0:T(8,128)(2,1)}, u32[]{:S(2)}) copy-start(bf16[512,128]{1,0:T(8,128)(2,1)} %down.1) | copy-start | bytes 393220

commit v8 on v7

--- a/solution.py
+++ b/solution.py
@@ -104,10 +104,10 @@
 
 
 def middle_kernel(
-    mixed, gates, fields, vectors, weight, out_weight, factors, fields_out, scratch, product
+    mixed, gates, fields, vectors, mixing, weight, out_weight, factors, fields_out, scratch, product
 ):
     gain, bias = vectors[:, 1:2], vectors[:, 4:5]
-    mix_gain, mix_bias = vectors[:, 6:7], vectors[:, 8:9]
+    mix_gain, mix_bias = mixing[:, 0:1], mixing[:, 2:3]
     field = finish(
         fields[...], take_mixed(mixed, product), mix_gain, mix_bias, out_weight[0].T, gates[...]
     )
@@ -116,9 +116,9 @@
     fields_out[...] = field
 
 
-def last_kernel(mixed, gates, fields, vectors, out_weight, up, down, updated, product):
+def last_kernel(mixed, gates, fields, vectors, mixing, out_weight, up, down, updated, product):
     gain, bias = vectors[:, 2:3], vectors[:, 5:6]
-    mix_gain, mix_bias = vectors[:, 7:8], vectors[:, 9:10]
+    mix_gain, mix_bias = mixing[:, 1:2], mixing[:, 3:4]
     inner = down.shape[0]
     field = finish(
         fields[...], take_mixed(mixed, product), mix_gain, mix_bias, out_weight[1].T, gates[...]
@@ -191,7 +191,7 @@
 
 
 def outgoing_own_kernel(
-    own, pair, norm_gain, norm_bias, out_gain, out_bias, weight,
+    own, pair, norm_gain, norm_bias, weight,
     left, own_product, gates, fields, vectors, right,
 ):
     for g in range(COLS // FOLD):
@@ -199,14 +199,15 @@
         left[:, lanes_from(g)] = flat_rows(rows_of(own, columns, 0))
         right[:, lanes_from(g)] = flat_rows(rows_of(own, columns, 1))
     send_product(dot_rows(left, right), own_product, range(PAIRS))
-    vectors[...] = columns_of((norm_gain, norm_bias, out_gain, out_bias))
+    vectors[...] = columns_of((norm_gain, norm_bias))
     field = field_of(pair)
     normed = layer_norm(field, vectors[:, 0:1], vectors[:, 3:4]).astype(BF16)
     gates[...] = sigmoid_of_double(dot(halved(weight[4 * WIDTH :]), normed))
     fields[...] = field
 
 
-def outgoing_kernel(other, left, own_product, product, right):
+def outgoing_kernel(other, left, own_product, out_gain, out_bias, product, mixing, right):
+    mixing[...] = columns_of((out_gain, out_bias))
     core = core_index()
     for g in range(COLS // FOLD):
         columns = [g * FOLD + i for i in range(FOLD)]
@@ -276,10 +277,13 @@
     factor, square = pltpu.VMEM(wide, BF16), pltpu.VMEM(square, BF16)
     left, own_product, gate, field, vectors = call(
         outgoing_own_kernel, (*outs, shape(WIDTH, WIDTH, dtype=F32)), [factor], "outgoing_own"
-    )(own, pair, norm_gain, norm_bias, out_gain, out_bias, first_weight)
-    mixed = call(outgoing_kernel, product, [factor], "outgoing")(other, left, own_product)
+    )(own, pair, norm_gain, norm_bias, first_weight)
+    square_f32 = shape(WIDTH, WIDTH, dtype=F32)
+    mixed, mixing = call(outgoing_kernel, (product, square_f32), [factor], "outgoing")(
+        other, left, own_product, out_gain, out_bias
+    )
     factors, field = call(middle_kernel, (packed, flat), [packing, unpacking], "middle")(
-        exchange(mixed), gate, field, vectors, proj_weight, out_weight
+        exchange(mixed), gate, field, vectors, mixing, proj_weight, out_weight
     )
     own = exchange(factors)
     other = swap_cores(own)
@@ -289,7 +293,7 @@
     )
     mixed = call(incoming_kernel, product, [square, factor], "incoming")(other, own_mixed)
     updated = call(last_kernel, shape(*blocks), [unpacking], "last")(
-        exchange(mixed), gate, field, vectors, out_weight, up_weight, down_weight
+        exchange(mixed), gate, field, vectors, mixing, out_weight, up_weight, down_weight
     )
     return updated.reshape(FOLD * STEPS, SIDE, WIDTH)
 

time: 113 us -> 114 us (level)
  transfers between devices with their start and end apart: 2 -> 2, of which waited for: 1 -> 2; matrix products, arithmetic and copies ran while one was open for 0% -> 0% of each run, Pallas kernels for 2% -> 2%
where the time goes in v8:
time: 114 us; the launch traced here: 113 us
  blocking collectives  102 us (89%)
  Pallas kernels  7.36 us (6%)
  local copies, waits for them, and re-layouts  2.48 us (2%)
  waiting for transfers between devices  1.56 us (1%)
    all_to_all x4, blocking collectives, exchange(): lax.all_to_all(values, ('row', 'col'), 0, 0, axis_index_groups=PARITY)  102 us
  transfers between devices with their start and end apart: 2, of which 2 were waited for; matrix products, arithmetic and copies ran while one was open for 0% of the time, Pallas kernels for 2%

profile of v8, /device:TPU:2, one launch (start us, length us, event | category | flops | bytes accessed | tf_op | source)
XLA Modules:
  0.0 113.3 jit_solution(6032647924843913199)
XLA Ops:
  0.0 0.0 slice-start
  0.0 0.9 slice-done
  0.9 0.2 copy.11
  1.1 0.0 copy-done.1
  1.1 0.5 copy-done.6
  1.6 0.2 copy-done.5
  1.8 0.9 first.1
  2.7 34.7 %all_to_all.20.own = bf16[128,16,128]{2,1,0:T(8,128)(2,1)S(1)} all-to-all(bf16[128,16,128]{2,1,0:T(8,128)(2,1)S(1)} %first.1), channel_id=1, replica_groups={{0,32,64,96,128,160,192,224,1,33,65,97,129,161,193,225,2,34,66,98,130,1..., dimensions={0} | all-to-all | bytes 1048576 | tf_op jit(solution)/shard_map/all_to_all | solution.py:27
  37.4 0.1 collective-permute-start
  37.5 0.0 copy-start.8
  37.5 1.2 %outgoing_own.1 = (bf16[256,512]{1,0:T(8,128)(2,1)S(1)}, bf16[64,8,128]{2,1,0:T(8,128)(2,1)S(1)}, f32[128,1024]{1,0:T(8,128)S(1)}, f32[128,1024]{1,0:T(8,128)S(1)}, f32[128,128]{1,0:T(8,128)S(1)}) custom-call(bf16[128,16,128]{2,1,0:T(8,128)(2,1)S(1)} %all_to_all.20.own, bf16[4,8,32,128]{3,2,1,0:T(8,128)(2,1)S(1)} %bitcast.8, f32[3,128]{1,0:T(4,128)S(1)} %copy-done.5, ...), custom_call_target="tpu_custom_call" | custom-call | tf_op jit(solution)/shard_map/outgoing_own/pallas_call | solution.py:278
  38.7 0.3 collective-permute-done.other
  39.0 0.0 copy-done.8
  39.0 0.7 copy-done.7
  39.7 0.6 outgoing.1
  40.3 0.0 copy-start
  40.3 0.0 copy-start.3
  40.3 20.9 %all_to_all.21.mixed = bf16[128,8,128]{2,1,0:T(8,128)(2,1)S(1)} all-to-all(bf16[128,8,128]{2,1,0:T(8,128)(2,1)S(1)} %get-tuple-element.18), channel_id=1, replica_groups={{0,32,64,96,128,160,192,224,1,33,65,97,129,161,193,225,2,34,66,98,130,1..., dimensions={0} | all-to-all | bytes 524288 | tf_op jit(solution)/shard_map/all_to_all | solution.py:27
  61.2 0.0 copy-done
  61.2 0.0 copy-done.3
  61.2 1.1 middle.1
  62.3 25.1 %all_to_all.22.own = bf16[128,16,128]{2,1,0:T(8,128)(2,1)S(1)} all-to-all(bf16[128,16,128]{2,1,0:T(8,128)(2,1)S(1)} %get-tuple-element.23), channel_id=1, replica_groups={{0,32,64,96,128,160,192,224,1,33,65,97,129,161,193,225,2,34,66,98,130,1..., dimensions={0} | all-to-all | bytes 1048576 | tf_op jit(solution)/shard_map/all_to_all | solution.py:27
  87.4 0.0 collective-permute-start.1
  87.4 0.7 incoming_own.1
  88.1 1.2 %collective-permute-done.1.other = bf16[128,16,128]{2,1,0:T(8,128)(2,1)S(1)} collective-permute-done((bf16[128,16,128]{2,1,0:T(8,128)(2,1)S(1)}, bf16[128,16,128]{2,1,0:T(8,128)(2,1)S(1)}, u32[]{:S(2)}, u32[]{:S(2)}) %collective-permute-start.1) | collective-permute-done | bytes 524320 | tf_op jit(solution)/shard_map/ppermute | solution.py:31
  89.3 0.8 incoming.1
  90.1 0.0 copy-start.2
  90.2 0.0 copy-start.4
  90.2 21.0 %all_to_all.23.mixed = bf16[128,8,128]{2,1,0:T(8,128)(2,1)S(1)} all-to-all(bf16[128,8,128]{2,1,0:T(8,128)(2,1)S(1)} %incoming.1), channel_id=1, replica_groups={{0,32,64,96,128,160,192,224,1,33,65,97,129,161,193,225,2,34,66,98,130,1..., dimensions={0} | all-to-all | bytes 524288 | tf_op jit(solution)/shard_map/all_to_all | solution.py:27
  111.2 0.0 copy-done.2
  111.2 0.0 copy-done.4
  111.2 2.1 %last.1 = bf16[4,8,32,128]{3,2,1,0:T(8,128)(2,1)} custom-call(bf16[128,8,128]{2,1,0:T(8,128)(2,1)S(1)} %all_to_all.23.mixed, f32[128,1024]{1,0:T(8,128)S(1)} %get-tuple-element.26.gates, f32[128,1024]{1,0:T(8,128)S(1)} %get-tuple-element.24.fields, f32[128,128]{1,0:T(8,128)S(1)} %get-tuple-element.21.vectors, f32[128,128]{1,0:T(8,128)S(1)} %get-tuple-element.22.mixing, ...), custom_call_target="tpu_custom_call" | custom-call | tf_op jit(solution)/shard_map/last/pallas_call | solution.py:295
  (5 shorter events, 0.0 us)
Async XLA Ops:
  0.0 0.9 slice-start
  0.0 1.1 copy-start.1
  0.9 0.7 copy-start.6
  1.1 0.7 copy-start.5
  37.4 1.6 %collective-permute-start = (bf16[128,8,128]{2,1,0:T(8,128)(2,1)S(1)}, bf16[128,8,128]{2,1,0:T(8,128)(2,1)S(1)}, u32[]{:S(2)}, u32[]{:S(2)}) collective-permute-start(bf16[128,8,128]{2,1,0:T(8,128)(2,1)S(1)} %slice.8), channel_id=1, source_target_pairs={{0,16},{16,0},{32,48},{48,32},{64,80},{80,64},{96,112},{112,96},{1... | collective-permute-start | bytes 786440 | tf_op jit(solution)/shard_map/ppermute | solution.py:31
  37.5 1.5 %copy-start.8 = (f32[2,128]{1,0:T(2,128)S(1)}, f32[2,128]{1,0:T(2,128)}, u32[]{:S(2)}) copy-start(f32[2,128]{1,0:T(2,128)} %out_bias.1) | copy-start | bytes 3076
  39.0 0.7 copy-start.7
  40.3 20.9 %copy-start = (bf16[2,128,640]{2,1,0:T(8,128)(2,1)S(1)}, bf16[2,128,640]{2,1,0:T(8,128)(2,1)}, u32[]{:S(2)}) copy-start(bf16[2,128,640]{2,1,0:T(8,128)(2,1)} %weight.3) | copy-start | bytes 983044
  40.3 20.9 %copy-start.3 = (bf16[2,128,128]{2,1,0:T(8,128)(2,1)S(1)}, bf16[2,128,128]{2,1,0:T(8,128)(2,1)}, u32[]{:S(2)}) copy-start(bf16[2,128,128]{2,1,0:T(8,128)(2,1)} %out_weight.3) | copy-start | bytes 196612
  87.4 1.9 %collective-permute-start.1 = (bf16[128,16,128]{2,1,0:T(8,128)(2,1)S(1)}, bf16[128,16,128]{2,1,0:T(8,128)(2,1)S(1)}, u32[]{:S(2)}, u32[]{:S(2)}) collective-permute-start(bf16[128,16,128]{2,1,0:T(8,128)(2,1)S(1)} %all_to_all.22.own), channel_id=1, source_target_pairs={{0,16},{16,0},{32,48},{48,32},{64,80},{80,64},{96,112},{112,96},{1... | collective-permute-start | bytes 1572872 | tf_op jit(solution)/shard_map/ppermute | solution.py:31
  90.1 21.1 %copy-start.2 = (bf16[128,1024]{1,0:T(8,128)(2,1)S(1)}, bf16[128,1024]{1,0:T(8,128)(2,1)}, u32[]{:S(2)}) copy-start(bf16[128,1024]{1,0:T(8,128)(2,1)} %up.1) | copy-start | bytes 786436
  90.2 21.0 %copy-start.4 = (bf16[512,128]{1,0:T(8,128)(2,1)S(1)}, bf16[512,128]{1,0:T(8,128)(2,1)}, u32[]{:S(2)}) copy-start(bf16[512,128]{1,0:T(8,128)(2,1)} %down.1) | copy-start | bytes 393220
